TPU v7x, 32 devices: a whole 2x2x4 slice. The times are simulated.
32 devices in a mesh: dp: 4 (over z), expert: 8 (over y, x, core).
Axes of the slice: x: 2, y: 2, z: 4, core: 2. Of those that a mesh axis runs over, the one named last changes fastest.
Arguments:
- tokens: bfloat16 [4096, 1664], P(('dp', 'expert')), may hold values from -6 to 6
- cotangent: bfloat16 [4096, 1664], P(('dp', 'expert')), may hold values from -6 to 6
- counts: int32 [4096], P(('dp', 'expert')), may hold values from 0 to 8
- picks: int32 [4, 8, 8], P('dp'), may hold values from 0 to 1023, as said below
- router: float32 [1664, 8], replicated, may hold values from -1 to 1
- w_in: bfloat16 [8, 1664, 4096], P('expert', None, 'dp'), may hold values from -0.15625 to 0.15625
- w_out: bfloat16 [8, 4096, 1664], P('expert', 'dp'), may hold values from -0.09375 to 0.09375
Outputs:
- grad_tokens: bfloat16 [4096, 1664], P(('dp', 'expert'))
- grad_w_in: bfloat16 [8, 1664, 4096], P('expert', None, 'dp')
- grad_w_out: bfloat16 [8, 4096, 1664], P('expert', 'dp')
- grad_router: float32 [1664, 8], replicated
Inputs may be any that keep to these rules, and one draw needn't show every extreme that they name: For each group and each expert, 8 distinct positions in increasing order; positions k * 128 to (k + 1) * 128 - 1 hold at most 2 of one expert's picks, and each expert takes exactly 2 from some such range in every group.
All inputs are finite; a program needn't handle non-finite values.
Results may differ from a plain program's by a relative error of at most 0.017.
Values may be sent and summed in bfloat16 or wider, within the bound.
A program may use at most 64 MiB of HBM per device.

v0:
```python
import jax
import jax.numpy as jnp
from jax import lax
from jax.sharding import PartitionSpec as P

SLOT = 2


def normal_cdf(values):
    return 0.5 * (1.0 + jax.scipy.special.erf(values * 0.7071067811865476))


def gelu_exact(values):
    return values * normal_cdf(values)


def gelu_slope(values):
    return normal_cdf(values) + values * jnp.exp(-0.5 * values * values) * 0.3989422804014327


def contract_rows(left, right):
    return lax.dot_general(
        left, right, (((0,), (0,)), ((), ())), preferred_element_type=jnp.float32
    )


def contract_cols(left, right):
    return lax.dot_general(
        left, right, (((1,), (1,)), ((), ())), preferred_element_type=jnp.float32
    )


def shards(tokens, cotangent, counts, picks, router, w_in, w_out):
    experts = lax.axis_size("expert")
    owner_index = lax.axis_index("expert")
    tok_count = tokens.shape[0]
    feat_width = tokens.shape[1]
    pick_plan = picks[0]
    capacity = pick_plan.shape[1]
    bounds = jnp.arange(experts + 1, dtype=jnp.int32) * tok_count
    before = jnp.sum((pick_plan[:, :, None] < bounds[None, None, :]).astype(jnp.int32), axis=1)
    firsts = before[:, :experts]
    amounts = before[:, 1:] - firsts
    slot_rank = jnp.arange(SLOT, dtype=jnp.int32)
    own_first = lax.dynamic_index_in_dim(firsts, owner_index, 1, keepdims=False)
    own_amount = lax.dynamic_index_in_dim(amounts, owner_index, 1, keepdims=False)
    own_valid = slot_rank[None, :] < own_amount[:, None]
    own_pick = jnp.minimum(own_first[:, None] + slot_rank[None, :], capacity - 1)
    own_local = jnp.where(
        own_valid, jnp.take_along_axis(pick_plan, own_pick, axis=1) - owner_index * tok_count, 0
    )
    flat_local = own_local.reshape(-1)
    flat_valid = own_valid.reshape(-1)
    logits = jnp.dot(tokens.astype(jnp.float32), router, precision=lax.Precision.HIGHEST)
    router_prob = jax.nn.softmax(logits, axis=-1)
    weight = jnp.maximum(counts, 1).astype(jnp.float32)
    scaled = (cotangent.astype(jnp.float32) / weight[:, None]).astype(jnp.bfloat16)
    slot_keep = flat_valid[:, None]
    send_x = jnp.where(slot_keep, tokens[flat_local], 0).reshape(experts, SLOT, feat_width)
    send_dy = jnp.where(slot_keep, scaled[flat_local], 0).reshape(experts, SLOT, feat_width)
    expert_ids = jnp.arange(experts, dtype=jnp.int32)[:, None]
    send_gate = jnp.where(own_valid, router_prob[own_local, expert_ids], 0.0).astype(jnp.bfloat16)
    recv_x, recv_dy, recv_gate = (
        lax.all_to_all(send_x, "expert", split_axis=0, concat_axis=0, tiled=True),
        lax.all_to_all(send_dy, "expert", split_axis=0, concat_axis=0, tiled=True),
        lax.all_to_all(send_gate, "expert", split_axis=0, concat_axis=0, tiled=True),
    )
    slab_x = recv_x.reshape(experts * SLOT, feat_width)
    slab_dy = recv_dy.reshape(experts * SLOT, feat_width)
    slab_gate = recv_gate.reshape(-1)
    block_in = w_in[0]
    block_out = w_out[0]
    part_x = lax.all_gather(slab_x, "dp", axis=0, tiled=True)
    part_dy = lax.all_gather(slab_dy, "dp", axis=0, tiled=True)
    part_gate = lax.all_gather(slab_gate, "dp", axis=0, tiled=True)
    pre_act = jnp.dot(part_x, block_in, preferred_element_type=jnp.float32)
    activated = gelu_exact(pre_act).astype(jnp.bfloat16)
    part_out = jnp.dot(activated, block_out, preferred_element_type=jnp.float32)
    dy_wide = part_dy.astype(jnp.float32)
    gate_part = jnp.sum(dy_wide * part_out, axis=-1)
    out_grad = (part_gate.astype(jnp.float32)[:, None] * dy_wide).astype(jnp.bfloat16)
    act_grad = contract_cols(out_grad, block_out)
    pre_grad = (act_grad * gelu_slope(pre_act)).astype(jnp.bfloat16)
    row_part = contract_cols(pre_grad, block_in)
    grad_in = contract_rows(part_x, pre_grad)
    grad_out = contract_rows(activated, out_grad)
    rows_all = row_part
    gates_all = gate_part
    grad_in, grad_out, rows_all, gates_all = (grad_in, grad_out, rows_all, gates_all)
    row_sum = lax.psum_scatter(rows_all.astype(jnp.bfloat16), "dp", scatter_dimension=0, tiled=True)
    gate_sum = lax.psum_scatter(gates_all, "dp", scatter_dimension=0, tiled=True)
    gate_grad = gate_sum.astype(jnp.bfloat16)
    back_x = row_sum.reshape(experts, SLOT, feat_width)
    back_gate = gate_grad.reshape(experts, SLOT)
    ret_x, ret_gate = (
        lax.all_to_all(back_x, "expert", split_axis=0, concat_axis=0, tiled=True),
        lax.all_to_all(back_gate, "expert", split_axis=0, concat_axis=0, tiled=True),
    )
    token_ids = jnp.arange(tok_count, dtype=jnp.int32)
    hit_table = (flat_local[None, :] == token_ids[:, None]) & flat_valid[None, :]
    expert_sum = jnp.dot(
        hit_table.astype(jnp.bfloat16),
        ret_x.reshape(experts * SLOT, feat_width),
        preferred_element_type=jnp.float32,
    )
    gate_terms = jnp.where(flat_valid, ret_gate.reshape(-1).astype(jnp.float32), 0.0).reshape(
        experts, SLOT
    )
    hit_cube = hit_table.reshape(tok_count, experts, SLOT).astype(jnp.float32)
    prob_grad = jnp.einsum("tes,es->te", hit_cube, gate_terms, precision=lax.Precision.HIGHEST)
    logit_grad = router_prob * (
        prob_grad - jnp.sum(router_prob * prob_grad, axis=-1, keepdims=True)
    )
    grad_tokens = (
        expert_sum + jnp.dot(logit_grad, router.T, precision=lax.Precision.HIGHEST)
    ).astype(jnp.bfloat16)
    router_term = jnp.dot(tokens.astype(jnp.float32).T, logit_grad, precision=lax.Precision.HIGHEST)
    grad_router = lax.psum(router_term, ("dp", "expert"))
    return (
        grad_tokens,
        grad_in.astype(jnp.bfloat16)[None],
        grad_out.astype(jnp.bfloat16)[None],
        grad_router,
    )


def solution(mesh):
    placed = (
        P(("dp", "expert"), None),
        P(("dp", "expert"), None),
        P(("dp", "expert")),
        P("dp", None, None),
        P(),
        P("expert", None, "dp"),
        P("expert", "dp", None),
    )
    return jax.shard_map(
        shards,
        mesh=mesh,
        in_specs=placed,
        out_specs=(
            P(("dp", "expert"), None),
            P("expert", None, "dp"),
            P("expert", "dp", None),
            P(),
        ),
        check_vma=False,
    )
```

profile of v0, /device:TPU:0, one launch (start us, length us, event | category | flops | bytes accessed | tf_op | source)
XLA Modules:
  0.0 181.0 jit_solution(15337615574425184981)
XLA Ops:
  7.2 0.8 maximum_convert_fusion
  8.1 0.9 convert_reduce_fusion
  9.1 0.2 dynamic-slice_reduce_fusion
  9.8 1.4 gather_fusion.3
  11.2 1.7 gather_fusion.2
  12.9 0.6 gather.34
  13.6 1.9 %divide_convert_fusion = bf16[128,1664]{1,0:T(8,128)(2,1)} fusion(bf16[128,1664]{1,0:T(8,128)(2,1)} %param.8, f32[128]{0:T(128)S(1)} %maximum_convert_fusion), kind=kLoop, calls=%fused_computation.24 | loop fusion | flops 638976 | bytes 852480 | tf_op jit(solution)/shard_map/convert_element_type | solution.py:57
  15.5 1.7 gather_fusion.1
  17.2 0.6 gather.32
  17.9 1.6 broadcast_select_fusion.1
  19.5 5.2 %all-to-all-start.1 = ((bf16[8,2,1664]{2,1,0:T(2,128)(2,1)}), bf16[8,2,1664]{2,1,0:T(2,128)(2,1)S(1)}, u32[]{:S(2)}, u32[]{:S(2)}) async-start(bf16[8,2,1664]{2,1,0:T(2,128)(2,1)} %get-tuple-element.8), calls=%async_computation.1 | async-start | bytes 106496 | tf_op jit(solution)/shard_map/all_to_all | solution.py:65
  25.0 1.4 fusion.59
  26.5 0.7 fusion.49
  27.1 0.6 lt.168
  27.8 0.7 add.133
  28.4 0.6 lt.170
  29.2 1.3 fusion.58
  31.9 4.2 %all-to-all-start.2 = ((bf16[8,2,1664]{2,1,0:T(2,128)(2,1)}), bf16[8,2,1664]{2,1,0:T(2,128)(2,1)S(1)}, u32[]{:S(2)}, u32[]{:S(2)}) async-start(bf16[8,2,1664]{2,1,0:T(2,128)(2,1)} %get-tuple-element.9), calls=%async_computation.2 | async-start | bytes 106496 | tf_op jit(solution)/shard_map/all_to_all | solution.py:64
  36.1 0.6 reshape.414
  36.8 16.1 %all_gather.10 = bf16[64,1664]{1,0:T(8,128)(2,1)} all-gather(bf16[16,1664]{1,0:T(8,128)(2,1)} %reshape.414), channel_id=1, replica_groups=mesh['dp'=4,'expert'=8] {'dp'}, dimensions={0}, use_global_device_ids=true | all-gather | bytes 266240 | tf_op jit(solution)/shard_map/all_gather | solution.py:74
  52.9 14.3 %all_gather.11 = bf16[64,1664]{1,0:T(8,128)(2,1)S(1)} all-gather(bf16[16,1664]{1,0:T(8,128)(2,1)S(1)} %reshape.415), channel_id=1, replica_groups=mesh['dp'=4,'expert'=8] {'dp'}, dimensions={0}, use_global_device_ids=true | all-gather | bytes 266240 | tf_op jit(solution)/shard_map/all_gather | solution.py:73
  67.3 0.7 copy-done.4
  67.9 0.7 fusion.2
  68.7 0.7 copy-done.2
  69.4 0.8 fusion.20
  70.2 10.1 %all-reduce.1 = bf16[64]{0:T(256)(128)(2,1)S(1)} all-reduce(f32[64]{0:T(128)S(1)} %fusion.20), channel_id=3, replica_groups=mesh['dp'=4,'expert'=8] {'dp'}, use_global_device_ids=true, to_apply=%region_5.6.clone | all-reduce | flops 64 | bytes 384
  80.4 8.5 %all_to_all.31 = bf16[8,1,2]{2,1,0:T(2,128)(2,1)S(1)} all-to-all(bf16[8,1,2]{2,1,0:T(2,128)(2,1)S(1)} %all_to_all.25), channel_id=1, replica_groups=mesh['dp'=4,'expert'=8] {'expert'}, dimensions={0} | all-to-all | bytes 64 | tf_op jit(solution)/shard_map/all_to_all | solution.py:97
  89.1 0.2 select_reduce_fusion
  89.4 0.7 gather_fusion
  90.2 0.1 copy.64
  90.3 0.1 copy.65
  90.4 7.0 %all_to_all.32 = bf16[8,1,2]{2,1,0:T(2,128)(2,1)S(1)} all-to-all(bf16[8,1,2]{2,1,0:T(2,128)(2,1)S(1)} %copy.65), channel_id=1, replica_groups=mesh['dp'=4,'expert'=8] {'expert'}, dimensions={0} | all-to-all | bytes 64 | tf_op jit(solution)/shard_map/all_to_all | solution.py:66
  97.5 0.2 dynamic-update-slice
  97.8 8.3 %all-reduce = bf16[64]{0:T(256)(128)(2,1)S(1)} all-reduce(bf16[64]{0:T(256)(128)(2,1)S(1)} %dynamic-update-slice), channel_id=1, replica_groups=mesh['dp'=4,'expert'=8] {'dp'}, use_global_device_ids=true, to_apply=%add | all-reduce | flops 64 | bytes 256
  106.1 0.5 copy-done.6
  106.6 3.2 %fusion.23 = bf16[64,1024]{1,0:T(8,128)(2,1)S(1)} fusion(bf16[1,1024,1664]{2,1,0:T(8,128)(2,1)} %param.13, f32[64,1024]{1,0:T(8,128)} %copy-done.2, bf16[64,1664]{1,0:T(8,128)(2,1)} %all_gather.10, f32[64]{0:T(128)S(1)} %convert_element_type.68), kind=kOutput, calls=%fused_computation.23 | convolution fusion | flops 219078656 | bytes 4014336 | tf_op jit(solution)/shard_map/dot_general | solution.py:28
  109.8 1.8 %fusion.14 = bf16[64,1664]{1,0:T(8,128)(2,1)} fusion(bf16[64,1024]{1,0:T(8,128)(2,1)S(1)} %fusion.23, bf16[1,1664,1024]{2,1,0:T(8,128)(2,1)S(1)} %copy-done), kind=kOutput, calls=%fused_computation.19 | convolution fusion | flops 218210304 | bytes 3751936 | tf_op jit(solution)/shard_map/dot_general | solution.py:28
  111.7 1.3 subtract_select_fusion
  113.0 1.9 %convolution_bitcast_fusion = f32[1664,8]{0,1:T(8,128)} fusion(bf16[128,1664]{1,0:T(8,128)(2,1)} %param.7, f32[128,8]{0,1:T(8,128)S(1)} %get-tuple-element.5, f32[8,128]{1,0:T(8,128)S(1)} %copy.79, f32[128]{0:T(128)S(1)} %get-tuple-element.4), kind=kOutput, calls=%fused_computation.20 | convolution fusion | flops 20449280 | bytes 487936 | tf_op jit(solution)/shard_map/dot_general | solution.py:117
  114.9 40.7 %psum.7 = f32[1664,8]{0,1:T(8,128)} all-reduce(f32[1664,8]{0,1:T(8,128)} %convolution_bitcast_fusion), channel_id=1, replica_groups=mesh['dp'=4,'expert'=8] {'dp','expert'}, use_global_device_ids=true, to_apply=%region_7.8 | all-reduce | flops 13312 | bytes 106496 | tf_op jit(solution)/shard_map/psum | solution.py:118
  155.6 3.9 %fusion.9 = bf16[1,1024,1664]{2,1,0:T(8,128)(2,1)} fusion(bf16[64,1664]{1,0:T(8,128)(2,1)} %all_gather.10, f32[64]{0:T(128)} %copy-done.6, f32[64,1024]{1,0:T(8,128)} %copy-done.2), kind=kOutput, calls=%fused_computation.15 | convolution fusion | flops 220454912 | bytes 3883264 | tf_op jit(solution)/shard_map/dot_general | solution.py:22
  159.6 1.5 reshape.416
  161.0 4.0 %all-to-all-start.3 = ((bf16[8,2,1664]{2,1,0:T(2,128)(2,1)}), bf16[8,2,1664]{2,1,0:T(2,128)(2,1)}, u32[]{:S(2)}, u32[]{:S(2)}) async-start(bf16[8,2,1664]{2,1,0:T(2,128)(2,1)} %reshape.416), calls=%async_computation.4 | async-start | bytes 106496 | tf_op jit(solution)/shard_map/all_to_all | solution.py:96
  165.0 3.8 %fusion.8 = bf16[1,1664,1024]{2,1,0:T(8,128)(2,1)} fusion(bf16[64,1664]{1,0:T(8,128)(2,1)} %copy-done.4, bf16[64,1024]{1,0:T(8,128)(2,1)S(1)} %fusion.23), kind=kOutput, calls=%fused_computation.14 | convolution fusion | flops 219807744 | bytes 3751936 | tf_op jit(solution)/shard_map/dot_general | solution.py:22
  168.7 1.2 all-to-all-done.3
  169.9 0.8 reshape.417
  170.8 0.9 fusion.36
  171.7 2.5 %fusion.10 = bf16[128,1664]{1,0:T(8,128)(2,1)} fusion(f32[128,1664]{1,0:T(8,128)S(1)} %fusion.36, f32[1664,8]{0,1:T(8,128)} %param.11, f32[128,8]{0,1:T(8,128)S(1)} %get-tuple-element.5, f32[8,128]{1,0:T(8,128)S(1)} %copy.79, f32[128]{0:T(128)S(1)} %get-tuple-element.4), kind=kOutput, calls=%fused_computation.17 | convolution fusion | flops 20875264 | bytes 1339904 | tf_op jit(solution)/shard_map/dot_general | solution.py:115
  (55 shorter events, 2.0 us)
Async XLA Ops:
  7.2 60.8 %copy-start = (bf16[1,1664,1024]{2,1,0:T(8,128)(2,1)S(1)}, bf16[1,1664,1024]{2,1,0:T(8,128)(2,1)}, u32[]{:S(2)}) copy-start(bf16[1,1664,1024]{2,1,0:T(8,128)(2,1)} %param.12) | copy-start | bytes 10223620
  7.2 17.8 %copy-start.5 = (f32[1664,8]{0,1:T(8,128)S(1)}, f32[1664,8]{0,1:T(8,128)}, u32[]{:S(2)}) copy-start(f32[1664,8]{0,1:T(8,128)} %param.11) | copy-start | bytes 159748
  19.5 12.4 %all-to-all-start.1 = ((bf16[8,2,1664]{2,1,0:T(2,128)(2,1)}), bf16[8,2,1664]{2,1,0:T(2,128)(2,1)S(1)}, u32[]{:S(2)}, u32[]{:S(2)}) async-start(bf16[8,2,1664]{2,1,0:T(2,128)(2,1)} %get-tuple-element.8), calls=%async_computation.1 | async-start | bytes 106496 | tf_op jit(solution)/shard_map/all_to_all | solution.py:65
  31.9 21.0 %all-to-all-start.2 = ((bf16[8,2,1664]{2,1,0:T(2,128)(2,1)}), bf16[8,2,1664]{2,1,0:T(2,128)(2,1)S(1)}, u32[]{:S(2)}, u32[]{:S(2)}) async-start(bf16[8,2,1664]{2,1,0:T(2,128)(2,1)} %get-tuple-element.9), calls=%async_computation.2 | async-start | bytes 106496 | tf_op jit(solution)/shard_map/all_to_all | solution.py:64
  36.1 123.5 %reduce-scatter.2.cloned.1.call-start = ((), (), s32[]{:S(2)}) async-start(), calls=%async_computation.6 | async-start | bytes 266240 | tf_op jit(solution)/shard_map/reduce_scatter | solution.py:90
  52.9 16.4 %copy-start.1 = (bf16[1,1024,1664]{2,1,0:T(8,128)(2,1)S(1)}, bf16[1,1024,1664]{2,1,0:T(8,128)(2,1)}, u32[]{:S(2)}) copy-start(bf16[1,1024,1664]{2,1,0:T(8,128)(2,1)} %param.13) | copy-start | bytes 10223620
  52.9 16.4 %copy-start.3 = (bf16[64,1664]{1,0:T(8,128)(2,1)S(1)}, bf16[64,1664]{1,0:T(8,128)(2,1)}, u32[]{:S(2)}) copy-start(bf16[64,1664]{1,0:T(8,128)(2,1)} %all_gather.10) | copy-start | bytes 638980
  67.2 0.7 copy-start.4
  67.9 21.5 %copy-start.8 = (f32[128]{0:T(128)S(1)}, f32[128]{0:T(128)}, u32[]{:S(2)}) copy-start(f32[128]{0:T(128)} %fusion.49) | copy-start | bytes 1540
  68.6 0.7 copy-start.2
  106.1 0.5 copy-start.6
  155.6 15.1 %copy-start.7 = (pred[16]{0:T(512)(128)(4,1)S(1)}, pred[16]{0:T(512)(128)(4,1)}, u32[]{:S(2)}) copy-start(pred[16]{0:T(512)(128)(4,1)} %lt.168) | copy-start | bytes 52
  161.0 8.9 %all-to-all-start.3 = ((bf16[8,2,1664]{2,1,0:T(2,128)(2,1)}), bf16[8,2,1664]{2,1,0:T(2,128)(2,1)}, u32[]{:S(2)}, u32[]{:S(2)}) async-start(bf16[8,2,1664]{2,1,0:T(2,128)(2,1)} %reshape.416), calls=%async_computation.4 | async-start | bytes 106496 | tf_op jit(solution)/shard_map/all_to_all | solution.py:96
Sparse Core Ops, SparseCore 0:
  111.8 17.2 reduce-scatter.1
where the time goes:
time: 182 us; the launch traced here: 181 us
  blocking collectives  105 us (58%)
  matrix products  21 us (12%)
  local copies, waits for them, and re-layouts  17 us (9%)
  between operations  15.5 us (9%)
  starting transfers between devices  13.4 us (7%)
  other arithmetic  7.79 us (4%)
    psum x1, blocking collectives, shards(): grad_router = lax.psum(router_term, ('dp', 'expert'))  40.7 us
    unnamed x2, blocking collectives  18.4 us
    all_gather x1, blocking collectives, shards(): part_dy = lax.all_gather(slab_dy, 'dp', axis=0, tiled=True)  16.1 us
    all_gather x1, blocking collectives, shards(): part_x = lax.all_gather(slab_x, 'dp', axis=0, tiled=True)  14.3 us
    all_to_all x1, blocking collectives, shards(): lax.all_to_all(back_gate, 'expert', split_axis=0, concat_axis=0, tiled=True)  8.53 us
    dot_general x2, matrix products, contract_rows(): lax.dot_general(left, right, (((0,), (0,)), ((), ())), preferred_element_...  7.68 us
    all_to_all x1, blocking collectives, shards(): lax.all_to_all(send_gate, 'expert', split_axis=0, concat_axis=0, tiled=True)  7.02 us
    all_to_all x1, starting transfers between devices, shards(): lax.all_to_all(send_dy, 'expert', split_axis=0, concat_axis=0, tiled=True)  5.17 us
  transfers between devices with their start and end apart: 4, of which 1 were waited for; matrix products, arithmetic and copies ran while one was open for 10% of the time, Pallas kernels for 0%

commit v1 on v0

v1 whole, which is shorter than its diff:
```python
import functools

import jax
import jax.numpy as jnp
from jax import lax
from jax.experimental import pallas as pl
from jax.experimental.pallas import tpu as pltpu
from jax.sharding import PartitionSpec as P

MESH = pl.DeviceIdType.MESH
BF16 = jnp.bfloat16
F32 = jnp.float32
SLOT = 2
SEG = 16
LANES = 128


def nn(left, right):
    return lax.dot_general(left, right, (((1,), (0,)), ((), ())), preferred_element_type=F32)


def nt(left, right):
    return lax.dot_general(left, right, (((1,), (1,)), ((), ())), preferred_element_type=F32)


def tn(left, right):
    return lax.dot_general(left, right, (((0,), (0,)), ((), ())), preferred_element_type=F32)


def iota(shape, dim):
    return lax.broadcasted_iota(jnp.int32, shape, dim)


def one_hot(mask):
    return jnp.where(mask, 1.0, 0.0).astype(BF16)


def split3(values):
    high = values.astype(BF16).astype(F32)
    rest = values - high
    mid = rest.astype(BF16).astype(F32)
    return high, mid, rest - mid


def normal_cdf(values):
    return 0.5 * (1.0 + lax.erf(values * 0.7071067811865476))


def exchange(axis, count, me, source, target, send_sem, recv_sem):
    copies = []
    for step in range(1, count):
        peer = lax.rem(me + step, count)
        copy = pltpu.make_async_remote_copy(
            src_ref=source(peer),
            dst_ref=target,
            send_sem=send_sem.at[step],
            recv_sem=recv_sem.at[step],
            device_id={axis: peer},
            device_id_type=MESH,
        )
        copy.start()
        copies.append(copy)
    return copies


def arrive(copies):
    for copy in copies:
        copy.wait_recv()


def route_kernel(
    experts, groups, tok_ref, cot_ref, cnt_ref, pick_ref, router_ref, win_hbm, wout_hbm,
    x_ref, og_ref, act_ref, pg_ref, gt_ref, gr_ref,
    win, wout, send, recv, pack, acc, rows_s, rows_r, gate_r, gate_s, gates, ret_s, ret_r,
    term_s, term_r, sum_r, fin_r,
    w_sem, d_ss, d_rs, p_ss, p_rs, g_ss, g_rs, e_ss, e_rs, r_ss, r_rs, b_ss, b_rs,
    t_ss, t_rs, s_ss, s_rs, f_ss, f_rs,
):
    me = lax.axis_index("expert")
    my_group = lax.axis_index("dp")
    toks, width = tok_ref.shape
    capacity = pick_ref.shape[1]
    hidden = win.shape[1]
    count = groups * capacity
    piece = send.shape[2]
    half = rows_s.shape[2]
    back = ret_s.shape[2]
    chunk = term_s.shape[2]

    barrier = pltpu.get_barrier_semaphore()
    for step in range(1, experts):
        pl.semaphore_signal(
            barrier, inc=1, device_id={"expert": lax.rem(me + step, experts)}, device_id_type=MESH
        )
    for step in range(1, groups):
        pl.semaphore_signal(
            barrier, inc=1, device_id={"dp": lax.rem(my_group + step, groups)}, device_id_type=MESH
        )
    load_in = pltpu.make_async_copy(win_hbm, win, w_sem.at[0])
    load_out = pltpu.make_async_copy(wout_hbm, wout, w_sem.at[1])
    load_in.start()
    load_out.start()

    tok = tok_ref[...]
    router = router_ref[...]
    stacked = jnp.concatenate(split3(router), axis=0).astype(BF16)
    parts = nt(stacked, tok)
    logits = parts[:experts] + parts[experts : 2 * experts] + parts[2 * experts :]
    raised = jnp.exp(logits - jnp.max(logits, axis=0, keepdims=True))
    prob = raised / jnp.sum(raised, axis=0, keepdims=True)
    weight_row = jnp.maximum(cnt_ref[...], 1).astype(F32)
    diagonal = iota((toks, toks), 0) == iota((toks, toks), 1)
    weight = jnp.sum(jnp.where(diagonal, weight_row, 0.0), axis=1, keepdims=True)
    scaled = (cot_ref[...].astype(F32) / weight).astype(BF16)

    picks = pick_ref[...]
    owner = picks // toks
    place = picks - owner * toks
    codes = jnp.concatenate([owner, place], axis=1).astype(F32).astype(BF16)
    wide = experts * SEG
    spread = one_hot(iota((wide, experts), 0) // SEG == iota((wide, experts), 1))
    spread_codes = nn(spread, codes)
    held = spread_codes[:, :capacity] == me.astype(F32)
    spots = spread_codes[:, capacity:]
    first = jnp.min(jnp.where(held, spots, 1e6), axis=1, keepdims=True)
    last = jnp.max(jnp.where(held, spots, -1.0), axis=1, keepdims=True)
    last = jnp.where(last > first, last, -1.0)
    seat = iota((wide, toks), 0) % SEG
    token_id = iota((wide, toks), 1).astype(F32)
    hit = (token_id == jnp.where(seat % SLOT == 0, first, last)).astype(F32)

    pieces = SEG // (2 * SLOT)
    total = jnp.zeros((wide, piece), F32)
    for part in range(pieces):
        low = part * piece
        high = min(width, low + piece)
        inside = seat // (2 * SLOT) == part
        late = seat % (2 * SLOT) >= SLOT
        take_x = jnp.where(inside & ~late, hit, 0.0).astype(BF16)
        take_dy = jnp.where(inside & late, hit, 0.0).astype(BF16)
        term = nn(take_x, tok[:, low:high]) + nn(take_dy, scaled[:, low:high])
        if part == pieces - 1:
            padded = jnp.concatenate([prob, jnp.zeros((LANES - experts, toks), F32)], axis=0)
            gate_cols = nt(take_dy, padded.astype(BF16))
            columns = [term, gate_cols]
            spare = piece - (high - low) - LANES
            if spare:
                columns.append(jnp.zeros((wide, spare), F32))
            term = jnp.concatenate(columns, axis=1)
        total = total + term
    send[...] = total.astype(BF16).reshape(experts, SEG, piece)
    recv[pl.ds(me, 1)] = send[pl.ds(me, 1)]

    pl.semaphore_wait(barrier, experts - 1 + groups - 1)
    dispatch = exchange("expert", experts, me, lambda peer: send.at[peer], recv.at[me], d_ss, d_rs)

    mine = iota((experts, capacity), 0) == me
    owner_row = jnp.sum(jnp.where(mine, owner, 0), axis=0, keepdims=True)
    tall = 2 * capacity
    slot_row = iota((tall, capacity), 0) % capacity
    slot_col = iota((tall, capacity), 1)
    owner_col = jnp.sum(jnp.where(slot_row == slot_col, owner_row, 0), axis=1, keepdims=True)
    same = owner_col == owner_row
    rank_col = jnp.sum(jnp.where(same & (slot_col < slot_row), 1, 0), axis=1, keepdims=True)
    seat_c = iota((tall, wide), 1) % SEG
    is_dy = jnp.where(iota((tall, wide), 0) >= capacity, 1, 0)
    wanted = (iota((tall, wide), 1) // SEG == owner_col) & (
        seat_c % (2 * SLOT) == SLOT * is_dy + rank_col
    )
    before = same[:capacity] & (slot_row[:capacity] < slot_col[:capacity])
    rank_row = jnp.sum(jnp.where(before, 1, 0), axis=0, keepdims=True)
    row_u = iota((wide, capacity), 0)
    from_owner = row_u // SEG == owner_row

    arrive(dispatch)
    rows_in = recv[...].reshape(wide, piece)
    packed = []
    for part in range(pieces):
        block = one_hot(wanted & (seat_c // (2 * SLOT) == part))
        packed.append(nn(block, rows_in).astype(BF16))
    whole = pack.shape[2]
    for part in range(pieces):
        low = part * piece
        high = min(whole, low + piece)
        pack[pl.ds(my_group, 1), :, low:high] = packed[part][None, :, : high - low]
    gather = exchange("dp", groups, my_group, lambda peer: pack.at[my_group], pack.at[my_group], p_ss, p_rs)
    arrive(gather)

    every = pack[...].astype(F32)
    x_rows = every[:, :capacity, :width].reshape(count, width).astype(BF16)
    dy_wide = every[:, capacity:, :width].reshape(count, width)
    gate_lanes = every[:, capacity:, width : width + LANES].reshape(count, LANES)
    lane = iota((count, LANES), 1)
    gate = jnp.sum(jnp.where(lane == me, gate_lanes, 0.0), axis=1, keepdims=True)
    dy_rows = dy_wide.astype(BF16)
    x_ref[...] = x_rows
    og_ref[...] = (gate * dy_wide).astype(BF16)

    load_in.wait()
    load_out.wait()
    step_cols = min(hidden, 256)
    gate_part = jnp.zeros((count, 1), F32)
    for tile in range(hidden // step_cols):
        cols = slice(tile * step_cols, (tile + 1) * step_cols)
        pre = nn(x_rows, win[:, cols])
        back_act = nt(dy_rows, wout[cols, :])
        cdf = normal_cdf(pre)
        act = (pre * cdf).astype(BF16)
        slope = cdf + pre * jnp.exp(-0.5 * pre * pre) * 0.3989422804014327
        act_ref[:, cols] = act
        pg_ref[:, cols] = (gate * back_act * slope).astype(BF16)
        gate_part = gate_part + jnp.sum(act.astype(F32) * back_act, axis=1, keepdims=True)
    gate_s[...] = jnp.broadcast_to(gate_part, (count, LANES)).reshape(groups, capacity, LANES)
    gate_r[pl.ds(my_group, 1)] = gate_s[pl.ds(my_group, 1)]
    gate_sum = exchange("dp", groups, my_group, lambda peer: gate_s.at[peer], gate_r.at[my_group], g_ss, g_rs)

    for tile in range(hidden // step_cols):
        cols = slice(tile * step_cols, (tile + 1) * step_cols)
        term = nt(pg_ref[:, cols], win[:, cols])
        if tile == 0:
            acc[...] = term
        else:
            acc[...] += term
    row_part = acc[...].reshape(groups, capacity, width)
    right = jnp.concatenate(
        [row_part[:, :, half:], jnp.zeros((groups, capacity, 2 * half - width), F32)], axis=2
    )
    rows_s[...] = jnp.concatenate([row_part[:, :, :half], right], axis=1).astype(BF16)
    rows_r[pl.ds(my_group, 1)] = rows_s[pl.ds(my_group, 1)]
    row_sum = exchange("dp", groups, my_group, lambda peer: rows_s.at[peer], rows_r.at[my_group], r_ss, r_rs)

    arrive(gate_sum)
    gate_total = gate_r[0]
    for group in range(1, groups):
        gate_total = gate_total + gate_r[group]
    gate_total = gate_total.astype(BF16).astype(F32)
    gate_total = jnp.where(iota((capacity, LANES), 1) == me, gate_total, 0.0)
    gates[pl.ds(me, 1)] = gate_total[None]
    gate_back = exchange("expert", experts, me, lambda peer: gates.at[me], gates.at[me], e_ss, e_rs)

    arrive(row_sum)
    row_total = rows_r[0].astype(F32)
    for group in range(1, groups):
        row_total = row_total + rows_r[group].astype(F32)
    row_grad = jnp.concatenate(
        [row_total[:capacity], row_total[capacity:, : width - half]], axis=1
    ).astype(BF16).astype(F32)
    returned = jnp.zeros((wide, back), F32)
    back_pieces = SEG // SLOT
    for part in range(back_pieces):
        low = part * back
        high = min(width, low + back)
        if high <= low:
            continue
        give = jnp.where(from_owner & (row_u % SEG == SLOT * part + rank_row), 1.0, 0.0)
        term = nn(give, row_grad[:, low:high])
        if high - low < back:
            term = jnp.concatenate([term, jnp.zeros((wide, back - high + low), F32)], axis=1)
        returned = returned + term
    ret_s[...] = returned.astype(BF16).reshape(experts, SEG, back)
    ret_r[pl.ds(me, 1)] = ret_s[pl.ds(me, 1)]
    give_back = exchange("expert", experts, me, lambda peer: ret_s.at[peer], ret_r.at[me], b_ss, b_rs)

    flat = experts * capacity
    spread_c = one_hot(iota((flat, experts), 0) // capacity == iota((flat, experts), 1))
    flat_codes = nn(spread_c, codes)
    own_pick = (iota((flat, capacity), 0) % capacity == iota((flat, capacity), 1)) & (
        flat_codes[:, :capacity] == me.astype(F32)
    )
    spot = jnp.sum(jnp.where(own_pick, flat_codes[:, capacity:] + 1.0, 0.0), axis=1, keepdims=True)
    at_token = one_hot(iota((flat, toks), 1).astype(F32) + 1.0 == spot)
    arrive(gate_back)
    gate_rows = gates[...].reshape(flat, LANES).astype(BF16)
    prob_grad = tn(gate_rows, at_token)[:experts]
    logit_grad = prob * (prob_grad - jnp.sum(prob * prob_grad, axis=0, keepdims=True))
    lg3 = jnp.concatenate(split3(logit_grad), axis=0).astype(BF16)
    terms = nn(lg3, tok)
    term = terms[:experts] + terms[experts : 2 * experts] + terms[2 * experts :]
    for part in range(experts):
        low = part * chunk
        high = min(width, low + chunk)
        if high <= low:
            term_s[part] = jnp.zeros((experts, chunk), F32)
            continue
        value = term[:, low:high]
        if high - low < chunk:
            value = jnp.concatenate([value, jnp.zeros((experts, chunk - high + low), F32)], axis=1)
        term_s[part] = value
    term_r[pl.ds(me, 1)] = term_s[pl.ds(me, 1)]
    scatter = exchange("expert", experts, me, lambda peer: term_s.at[peer], term_r.at[me], t_ss, t_rs)

    r1, r2, r3 = split3(router)
    l1, l2, l3 = split3(logit_grad)
    left = jnp.concatenate([l1, l1, l2, l1, l3, l2], axis=0).astype(BF16)
    near = jnp.concatenate([r1, r2, r1, r3, r1, r2], axis=0).astype(BF16)
    gt_wide = tn(left, near)

    arrive(scatter)
    term_sum = term_r[0]
    for part in range(1, experts):
        term_sum = term_sum + term_r[part]
    sum_r[pl.ds(my_group, 1)] = term_sum[None]
    over_dp = exchange("dp", groups, my_group, lambda peer: sum_r.at[my_group], sum_r.at[my_group], s_ss, s_rs)

    arrive(give_back)
    ret_rows = ret_r[...].reshape(wide, back)
    for part in range(back_pieces):
        low = part * back
        high = min(width, low + back)
        if high <= low:
            continue
        mark = jnp.where(seat // SLOT == part, hit, 0.0).astype(BF16)
        expert_sum = tn(mark, ret_rows[:, : high - low])
        gt_ref[:, low:high] = (expert_sum + gt_wide[:, low:high]).astype(BF16)

    arrive(over_dp)
    final = sum_r[0]
    for group in range(1, groups):
        final = final + sum_r[group]
    fin_r[pl.ds(me, 1)] = final[None]
    spread_out = exchange("expert", experts, me, lambda peer: fin_r.at[me], fin_r.at[me], f_ss, f_rs)
    arrive(spread_out)
    for part in range(experts):
        low = part * chunk
        high = min(width, low + chunk)
        if high > low:
            gr_ref[:, low:high] = fin_r[part][:, : high - low]
    for copies in (
        dispatch, gather, gate_sum, row_sum, gate_back, give_back, scatter, over_dp, spread_out
    ):
        for copy in copies:
            copy.wait_send()


def weight_kernel(x_ref, og_ref, act_ref, pg_ref, gin_ref, gout_ref):
    gin_ref[0] = tn(x_ref[...], pg_ref[...]).astype(BF16)
    gout_ref[0] = tn(act_ref[...], og_ref[...]).astype(BF16)


def shards(experts, groups, tokens, cotangent, counts, picks, router, w_in, w_out):
    toks, width = tokens.shape
    capacity = picks.shape[2]
    hidden = w_in.shape[2]
    count = groups * capacity
    tiles = -(-width // LANES)
    pieces = SEG // (2 * SLOT)
    piece = LANES * -(-(tiles + 1) // pieces)
    whole = width + LANES
    half = LANES * -(-tiles // 2)
    back = LANES * -(-tiles // (SEG // SLOT))
    chunk = LANES * -(-tiles // experts)
    vmem = pl.BlockSpec(memory_space=pltpu.VMEM)
    hbm = pl.BlockSpec(memory_space=pl.ANY)
    dma = pltpu.SemaphoreType.DMA
    over_e, over_g = dma((experts,)), dma((groups,))
    x_rows, out_grad, act, pre_grad, grad_tokens, grad_router = pl.pallas_call(
        functools.partial(route_kernel, experts, groups),
        out_shape=(
            jax.ShapeDtypeStruct((count, width), BF16),
            jax.ShapeDtypeStruct((count, width), BF16),
            jax.ShapeDtypeStruct((count, hidden), BF16),
            jax.ShapeDtypeStruct((count, hidden), BF16),
            jax.ShapeDtypeStruct((toks, width), BF16),
            jax.ShapeDtypeStruct((experts, width), F32),
        ),
        in_specs=[vmem] * 5 + [hbm] * 2,
        out_specs=(vmem,) * 6,
        scratch_shapes=[
            pltpu.VMEM((width, hidden), BF16),
            pltpu.VMEM((hidden, width), BF16),
            pltpu.VMEM((experts, SEG, piece), BF16),
            pltpu.VMEM((experts, SEG, piece), BF16),
            pltpu.VMEM((groups, 2 * capacity, whole), BF16),
            pltpu.VMEM((count, width), F32),
            pltpu.VMEM((groups, 2 * capacity, half), BF16),
            pltpu.VMEM((groups, 2 * capacity, half), BF16),
            pltpu.VMEM((groups, capacity, LANES), F32),
            pltpu.VMEM((groups, capacity, LANES), F32),
            pltpu.VMEM((experts, capacity, LANES), F32),
            pltpu.VMEM((experts, SEG, back), BF16),
            pltpu.VMEM((experts, SEG, back), BF16),
            pltpu.VMEM((experts, experts, chunk), F32),
            pltpu.VMEM((experts, experts, chunk), F32),
            pltpu.VMEM((groups, experts, chunk), F32),
            pltpu.VMEM((experts, experts, chunk), F32),
            dma((2,)),
            over_e, over_e,
            over_g, over_g,
            over_g, over_g,
            over_e, over_e,
            over_g, over_g,
            over_e, over_e,
            over_e, over_e,
            over_g, over_g,
            over_e, over_e,
        ],
        compiler_params=pltpu.CompilerParams(
            collective_id=0, has_side_effects=True, vmem_limit_bytes=48 * 1024 * 1024
        ),
        name="route",
    )(tokens, cotangent, counts.reshape(1, toks), picks[0], router.T, w_in[0], w_out[0])

    cols = min(hidden, 256)
    grad_in, grad_out = pl.pallas_call(
        weight_kernel,
        grid=(hidden // cols,),
        out_shape=(
            jax.ShapeDtypeStruct((1, width, hidden), BF16),
            jax.ShapeDtypeStruct((1, hidden, width), BF16),
        ),
        in_specs=[
            pl.BlockSpec((count, width), lambda i: (0, 0)),
            pl.BlockSpec((count, width), lambda i: (0, 0)),
            pl.BlockSpec((count, cols), lambda i: (0, i)),
            pl.BlockSpec((count, cols), lambda i: (0, i)),
        ],
        out_specs=(
            pl.BlockSpec((1, width, cols), lambda i: (0, 0, i)),
            pl.BlockSpec((1, cols, width), lambda i: (0, i, 0)),
        ),
        compiler_params=pltpu.CompilerParams(vmem_limit_bytes=32 * 1024 * 1024),
        name="weight_grads",
    )(x_rows, out_grad, act, pre_grad)
    return grad_tokens, grad_in, grad_out, grad_router.T


def solution(mesh):
    placed = (
        P(("dp", "expert"), None),
        P(("dp", "expert"), None),
        P(("dp", "expert")),
        P("dp", None, None),
        P(),
        P("expert", None, "dp"),
        P("expert", "dp", None),
    )
    return jax.shard_map(
        functools.partial(shards, mesh.shape["expert"], mesh.shape["dp"]),
        mesh=mesh,
        in_specs=placed,
        out_specs=(
            P(("dp", "expert"), None),
            P("expert", None, "dp"),
            P("expert", "dp", None),
            P(),
        ),
        check_vma=False,
    )
```

time: 182 us -> 48.6 us (0.27)
  blocking collectives: 105 us -> 0 us
  Pallas kernels: 0 us -> 40.1 us
  matrix products: 21 us -> 0 us
  between operations: 15.5 us -> 0.66 us
  starting transfers between devices: 13.4 us -> 0 us
  local copies, waits for them, and re-layouts: 17 us -> 7.5 us
  other arithmetic: 7.79 us -> 0 us
    psum x1 -> x0, blocking collectives: 40.7 us -> none  [shards(): grad_router = lax.psum(router_term, ('dp', 'expert'))]
    pallas_call x0 -> x2, Pallas kernels: none -> 40.1 us  [the longest x1 35.7 us: shards(): pl.pallas_call(functools.partial(route_kernel, experts, groups), out_shap...]
    all_gather x2 -> x0, blocking collectives: 30.4 us -> none  [the longest x1 16.1 us: shards(): part_dy = lax.all_gather(slab_dy, 'dp', axis=0, tiled=True)]
    dot_general x10 -> x0, matrix products: 21 us -> none  [the longest x2 7.68 us: contract_rows(): lax.dot_general(left, right, (((0,), (0,)), ((), ())), preferred_element_...]
    unnamed x2 -> x0, blocking collectives: 18.4 us -> none
    all_to_all x2 -> x0, blocking collectives: 15.6 us -> none  [the longest x1 8.53 us: shards(): lax.all_to_all(back_gate, 'expert', split_axis=0, concat_axis=0, tiled=True)]
    all_to_all x3 -> x0, starting transfers between devices: 13.3 us -> none  [the longest x1 5.17 us: shards(): lax.all_to_all(send_dy, 'expert', split_axis=0, concat_axis=0, tiled=True)]
    gather x12 -> x0, local copies, waits for them, and re-layouts: 7.24 us -> none  [the longest x2 2.36 us: shards(): tokens[flat_local]]
  transfers between devices with their start and end apart: 4 -> 0, of which waited for: 1 -> 0; matrix products, arithmetic and copies ran while one was open for 10% -> 0% of each run, Pallas kernels for 0% -> 0%
where the time goes in v1:
time: 48.6 us; the launch traced here: 48.2 us
  Pallas kernels  40.1 us (83%)
  local copies, waits for them, and re-layouts  7.5 us (15%)
  between operations  0.66 us (1%)
    pallas_call x1, Pallas kernels, shards(): pl.pallas_call(functools.partial(route_kernel, experts, groups), out_shap...  35.7 us
    unnamed x14, local copies, waits for them, and re-layouts  7.5 us
    pallas_call x1, Pallas kernels, shards(): pl.pallas_call(weight_kernel, grid=(hidden // cols,), out_shape=(jax.Shap...  4.33 us

profile of v1, /device:TPU:0, one launch (start us, length us, event | category | flops | bytes accessed | tf_op | source)
XLA Modules:
  0.0 48.2 jit_solution(5567936343373193670)
XLA Ops:
  0.6 0.0 copy-start
  0.6 2.0 %copy-done = bf16[1,1664,1024]{2,1,0:T(8,128)(2,1)S(1)} copy-done((bf16[1,1664,1024]{2,1,0:T(8,128)(2,1)S(1)}, bf16[1,1664,1024]{2,1,0:T(8,128)(2,1)}, u32[]{:S(2)}) %copy-start) | copy-done | bytes 3407896
  2.6 0.0 copy-start.1
  2.6 1.0 %copy-done.1 = bf16[128,1664]{1,0:T(8,128)(2,1)S(1)} copy-done((bf16[128,1664]{1,0:T(8,128)(2,1)S(1)}, bf16[128,1664]{1,0:T(8,128)(2,1)}, u32[]{:S(2)}) %copy-start.1) | copy-done | bytes 426008
  3.6 0.0 copy-start.2
  3.6 1.0 %copy-done.2 = bf16[128,1664]{1,0:T(8,128)(2,1)S(1)} copy-done((bf16[128,1664]{1,0:T(8,128)(2,1)S(1)}, bf16[128,1664]{1,0:T(8,128)(2,1)}, u32[]{:S(2)}) %copy-start.2) | copy-done | bytes 426008
  4.6 0.0 copy-start.3
  4.6 0.8 %copy-done.3 = f32[1664,8]{0,1:T(8,128)S(1)} copy-done((f32[1664,8]{0,1:T(8,128)S(1)}, f32[1664,8]{0,1:T(8,128)}, u32[]{:S(2)}) %copy-start.3) | copy-done | bytes 53272
  5.4 0.0 copy-start.4
  5.4 0.7 %copy-done.4 = s32[1,8,8]{2,1,0:T(8,128)S(1)} copy-done((s32[1,8,8]{2,1,0:T(8,128)S(1)}, s32[1,8,8]{2,1,0:T(8,128)}, u32[]{:S(2)}) %copy-start.4) | copy-done | bytes 280
  6.1 0.0 copy-start.5
  6.1 0.7 %copy-done.5 = s32[128]{0:T(128)S(1)} copy-done((s32[128]{0:T(128)S(1)}, s32[128]{0:T(128)}, u32[]{:S(2)}) %copy-start.5) | copy-done | bytes 536
  6.8 35.7 %route.1 = (bf16[32,1664]{1,0:T(8,128)(2,1)S(1)}, bf16[32,1664]{1,0:T(8,128)(2,1)S(1)}, bf16[32,1024]{1,0:T(8,128)(2,1)S(1)}, bf16[32,1024]{1,0:T(8,128)(2,1)S(1...) custom-call(bf16[128,1664]{1,0:T(8,128)(2,1)S(1)} %copy-done.1, bf16[128,1664]{1,0:T(8,128)(2,1)S(1)} %copy-done.2, ...), custom_call_target="tpu_custom_call" | custom-call | tf_op jit(solution)/shard_map/route/pallas_call | solution.py:356
  42.5 4.3 %weight_grads.1 = (bf16[1,1664,1024]{2,1,0:T(8,128)(2,1)}, bf16[1,1024,1664]{2,1,0:T(8,128)(2,1)}) custom-call(bf16[32,1664]{1,0:T(8,128)(2,1)S(1)} %get-tuple-element.13.x_ref, bf16[32,1664]{1,0:T(8,128)(2,1)S(1)} %get-tuple-element.14.og_ref, bf16[32,1024]{1,0:T(8,128)(2,1)S(1)} %get-tuple-element.15.act_ref, bf16[32,1024]{1,0:T(8,128)(2,1)S(1)} %get-tuple-element.16.pg_ref), custom_call_target="tpu_custom_call" | custom-call | tf_op jit(solution)/shard_map/weight_grads/pallas_call | solution.py:404
  46.8 0.8 %copy.13 = bf16[128,1664]{1,0:T(8,128)(2,1)} copy(bf16[128,1664]{1,0:T(8,128)(2,1)S(1)} %get-tuple-element.24) | data formatting | bytes 851968
  47.6 0.6 %copy.14 = f32[1664,8]{0,1:T(8,128)} copy(f32[1664,8]{0,1:T(8,128)S(1)} %bitcast.8) | data formatting | bytes 106496
Async XLA Ops:
  0.6 2.0 %copy-start = (bf16[1,1664,1024]{2,1,0:T(8,128)(2,1)S(1)}, bf16[1,1664,1024]{2,1,0:T(8,128)(2,1)}, u32[]{:S(2)}) copy-start(bf16[1,1664,1024]{2,1,0:T(8,128)(2,1)} %param.12) | copy-start | bytes 10223620
  2.6 1.0 %copy-start.1 = (bf16[128,1664]{1,0:T(8,128)(2,1)S(1)}, bf16[128,1664]{1,0:T(8,128)(2,1)}, u32[]{:S(2)}) copy-start(bf16[128,1664]{1,0:T(8,128)(2,1)} %tok_ref.1) | copy-start | bytes 1277956
  3.6 1.0 %copy-start.2 = (bf16[128,1664]{1,0:T(8,128)(2,1)S(1)}, bf16[128,1664]{1,0:T(8,128)(2,1)}, u32[]{:S(2)}) copy-start(bf16[128,1664]{1,0:T(8,128)(2,1)} %cot_ref.1) | copy-start | bytes 1277956
  4.6 0.8 %copy-start.3 = (f32[1664,8]{0,1:T(8,128)S(1)}, f32[1664,8]{0,1:T(8,128)}, u32[]{:S(2)}) copy-start(f32[1664,8]{0,1:T(8,128)} %param.11) | copy-start | bytes 159748
  5.4 0.7 %copy-start.4 = (s32[1,8,8]{2,1,0:T(8,128)S(1)}, s32[1,8,8]{2,1,0:T(8,128)}, u32[]{:S(2)}) copy-start(s32[1,8,8]{2,1,0:T(8,128)} %param.10) | copy-start | bytes 772
  6.1 0.7 %copy-start.5 = (s32[128]{0:T(128)S(1)}, s32[128]{0:T(128)}, u32[]{:S(2)}) copy-start(s32[128]{0:T(128)} %param.9) | copy-start | bytes 1540

commit v2 on v1

v2 whole, which is shorter than its diff:
```python
import functools

import jax
import jax.numpy as jnp
from jax import lax
from jax.experimental import pallas as pl
from jax.experimental.pallas import tpu as pltpu
from jax.sharding import PartitionSpec as P

MESH = pl.DeviceIdType.MESH
BF16 = jnp.bfloat16
F32 = jnp.float32
SLOT = 2
SEG = 16
LANES = 128


def nn(left, right):
    return lax.dot_general(left, right, (((1,), (0,)), ((), ())), preferred_element_type=F32)


def nt(left, right):
    return lax.dot_general(left, right, (((1,), (1,)), ((), ())), preferred_element_type=F32)


def tn(left, right):
    return lax.dot_general(left, right, (((0,), (0,)), ((), ())), preferred_element_type=F32)


def iota(shape, dim):
    return lax.broadcasted_iota(jnp.int32, shape, dim)


def one_hot(mask):
    return jnp.where(mask, 1.0, 0.0).astype(BF16)


def split3(values):
    high = values.astype(BF16).astype(F32)
    rest = values - high
    mid = rest.astype(BF16).astype(F32)
    return high, mid, rest - mid


def normal_cdf(values):
    return 0.5 * (1.0 + lax.erf(values * 0.7071067811865476))


def exchange(axis, count, me, source, target, send_sem, recv_sem):
    copies = []
    for step in range(1, count):
        peer = lax.rem(me + step, count)
        copy = pltpu.make_async_remote_copy(
            src_ref=source(peer),
            dst_ref=target,
            send_sem=send_sem.at[step],
            recv_sem=recv_sem.at[step],
            device_id={axis: peer},
            device_id_type=MESH,
        )
        copy.start()
        copies.append(copy)
    return copies


def arrive(copies):
    for copy in copies:
        copy.wait_recv()


def route_kernel(
    experts, groups, tok_hbm, cot_hbm, cnt_hbm, pick_hbm, router_hbm, win_hbm, wout_hbm,
    x_hbm, og_hbm, act_hbm, pg_hbm, gt_hbm, gr_hbm,
    x_ref, og_ref, gt_ref, gr_ref, tok_ref, cot_ref, cnt_ref, pick_ref, router_ref, win, wout,
    send, recv, pack, act_ref, pg_ref, acc, rows_s, rows_r, ret_s, ret_r,
    term_s, term_r, sum_r, fin_r,
    in_sem, out_sem, d_ss, d_rs, p_ss, p_rs, r_ss, r_rs, b_ss, b_rs, t_ss, t_rs, s_ss, s_rs, f_ss, f_rs,
):
    me = lax.axis_index("expert")
    my_group = lax.axis_index("dp")
    toks, width = tok_ref.shape
    capacity = pick_ref.shape[1]
    hidden = win.shape[1]
    count = groups * capacity
    piece = send.shape[2]
    half = rows_s.shape[2]
    back = ret_s.shape[2]
    chunk = term_s.shape[2]

    barrier = pltpu.get_barrier_semaphore()
    for step in range(1, experts):
        pl.semaphore_signal(
            barrier, inc=1, device_id={"expert": lax.rem(me + step, experts)}, device_id_type=MESH
        )
    for step in range(1, groups):
        pl.semaphore_signal(
            barrier, inc=1, device_id={"dp": lax.rem(my_group + step, groups)}, device_id_type=MESH
        )
    loads = []
    for source, target in (
        (pick_hbm, pick_ref), (tok_hbm, tok_ref), (router_hbm, router_ref), (cnt_hbm, cnt_ref),
        (cot_hbm, cot_ref), (win_hbm, win), (wout_hbm, wout),
    ):
        loads.append(pltpu.make_async_copy(source, target, in_sem.at[len(loads)]))
    stores = []
    for source, target in (
        (x_ref, x_hbm), (og_ref, og_hbm), (act_ref, act_hbm), (pg_ref, pg_hbm), (gt_ref, gt_hbm), (gr_ref, gr_hbm)
    ):
        stores.append(pltpu.make_async_copy(source, target, out_sem.at[len(stores)]))
    load_pick, load_tok, load_router, load_cnt, load_cot, load_in, load_out = loads
    for load in loads[:5]:
        load.start()

    load_pick.wait()
    picks = pick_ref[...]
    owner = picks // toks
    place = picks - owner * toks
    codes = jnp.concatenate([owner, place], axis=1).astype(F32).astype(BF16)
    wide = experts * SEG
    spread = one_hot(iota((wide, experts), 0) // SEG == iota((wide, experts), 1))
    spread_codes = nn(spread, codes)
    held = spread_codes[:, :capacity] == me.astype(F32)
    spots = spread_codes[:, capacity:]
    first = jnp.min(jnp.where(held, spots, 1e6), axis=1, keepdims=True)
    last = jnp.max(jnp.where(held, spots, -1.0), axis=1, keepdims=True)
    last = jnp.where(last > first, last, -1.0)
    seat = iota((wide, toks), 0) % SEG
    token_id = iota((wide, toks), 1).astype(F32)
    hit = (token_id == jnp.where(seat % SLOT == 0, first, last)).astype(F32)
    late = seat % (2 * SLOT) >= SLOT
    take = jnp.concatenate([jnp.where(late, 0.0, hit), jnp.where(late, hit, 0.0)], axis=1)
    part_of = iota((wide, 2 * toks), 0) % SEG // (2 * SLOT)

    load_tok.wait()
    load_router.wait()
    tok = tok_ref[...]
    router = router_ref[...]
    stacked = jnp.concatenate(split3(router), axis=0).astype(BF16)
    parts = nt(stacked, tok)
    load_cnt.wait()
    load_cot.wait()
    load_in.start()
    load_out.start()
    weight_row = jnp.maximum(cnt_ref[...], 1).astype(F32)
    diagonal = iota((toks, toks), 0) == iota((toks, toks), 1)
    weight = jnp.sum(jnp.where(diagonal, weight_row, 0.0), axis=1, keepdims=True)
    scaled = (cot_ref[...].astype(F32) / weight).astype(BF16)
    logits = parts[:experts] + parts[experts : 2 * experts] + parts[2 * experts :]
    raised = jnp.exp(logits - jnp.max(logits, axis=0, keepdims=True))
    prob = raised / jnp.sum(raised, axis=0, keepdims=True)

    pieces = SEG // (2 * SLOT)
    both = jnp.concatenate([tok, scaled], axis=0)
    total = jnp.zeros((wide, piece), F32)
    for part in range(pieces):
        low = part * piece
        high = min(width, low + piece)
        chosen = jnp.where(part_of == part, take, 0.0).astype(BF16)
        term = nn(chosen, both[:, low:high])
        if part == pieces - 1:
            padded = jnp.concatenate(
                split3(prob) + (jnp.zeros((LANES - 3 * experts, toks), F32),), axis=0
            )
            columns = [term, nt(chosen[:, toks:], padded.astype(BF16))]
            spare = piece - (high - low) - LANES
            if spare:
                columns.append(jnp.zeros((wide, spare), F32))
            term = jnp.concatenate(columns, axis=1)
        total = total + term
    send[...] = total.astype(BF16).reshape(experts, SEG, piece)
    recv[pl.ds(me, 1)] = send[pl.ds(me, 1)]

    pl.semaphore_wait(barrier, experts - 1 + groups - 1)
    dispatch = exchange("expert", experts, me, lambda peer: send.at[peer], recv.at[me], d_ss, d_rs)

    mine = iota((experts, capacity), 0) == me
    owner_row = jnp.sum(jnp.where(mine, owner, 0), axis=0, keepdims=True)
    tall = 2 * capacity
    slot_row = iota((tall, capacity), 0) % capacity
    slot_col = iota((tall, capacity), 1)
    owner_col = jnp.sum(jnp.where(slot_row == slot_col, owner_row, 0), axis=1, keepdims=True)
    same = owner_col == owner_row
    rank_col = jnp.sum(jnp.where(same & (slot_col < slot_row), 1, 0), axis=1, keepdims=True)
    seat_c = iota((tall, wide), 1) % SEG
    is_dy = jnp.where(iota((tall, wide), 0) >= capacity, 1, 0)
    wanted = (iota((tall, wide), 1) // SEG == owner_col) & (
        seat_c % (2 * SLOT) == SLOT * is_dy + rank_col
    )
    blocks = [one_hot(wanted & (seat_c // (2 * SLOT) == part)) for part in range(pieces)]
    before = same[:capacity] & (slot_row[:capacity] < slot_col[:capacity])
    rank_row = jnp.sum(jnp.where(before, 1, 0), axis=0, keepdims=True)
    row_u = iota((wide, capacity), 0)
    from_owner = row_u // SEG == owner_row
    hit_turned = hit.T
    seat_turned = iota((toks, wide), 1) % SEG

    arrive(dispatch)
    rows_in = recv[...].reshape(wide, piece)
    whole = pack.shape[2]
    for part in range(pieces):
        low = part * piece
        high = min(whole, low + piece)
        packed = nn(blocks[part], rows_in[:, : high - low]).astype(BF16)
        pack[pl.ds(my_group, 1), :, low:high] = packed[None]
    gather = exchange("dp", groups, my_group, lambda peer: pack.at[my_group], pack.at[my_group], p_ss, p_rs)
    load_in.wait()
    load_out.wait()
    arrive(gather)

    every = pack[...].astype(F32)
    x_rows = every[:, :capacity, :width].reshape(count, width).astype(BF16)
    dy_wide = every[:, capacity:, :width].reshape(count, width)
    gate_lanes = every[:, capacity:, width : width + LANES].reshape(count, LANES)
    lane = iota((count, LANES), 1)
    gate = jnp.sum(jnp.where(lane == me, gate_lanes, 0.0), axis=1, keepdims=True)
    dy_rows = dy_wide.astype(BF16)
    x_ref[...] = x_rows
    og_ref[...] = (gate * dy_wide).astype(BF16)
    stores[0].start()
    stores[1].start()

    step_cols = min(hidden, 256)
    gate_part = jnp.zeros((count, 1), F32)
    for tile in range(hidden // step_cols):
        cols = slice(tile * step_cols, (tile + 1) * step_cols)
        pre = nn(x_rows, win[:, cols])
        back_act = nt(dy_rows, wout[cols, :])
        cdf = normal_cdf(pre)
        act = (pre * cdf).astype(BF16)
        slope = cdf + pre * jnp.exp(-0.5 * pre * pre) * 0.3989422804014327
        act_ref[:, cols] = act
        pg_ref[:, cols] = (gate * back_act * slope).astype(BF16)
        gate_part = gate_part + jnp.sum(act.astype(F32) * back_act, axis=1, keepdims=True)

    stores[2].start()
    stores[3].start()

    fold_row, fold_col = iota((LANES, LANES), 0), iota((LANES, LANES), 1)
    fold = one_hot((fold_row % experts == fold_col) & (fold_row < 3 * experts))
    row_prob = nn(gate_lanes.astype(BF16), fold)
    own_prob = jnp.sum(jnp.where(lane == me, row_prob, 0.0), axis=1, keepdims=True)
    logit_part = gate_part * row_prob * (jnp.where(lane == me, 1.0, 0.0) - own_prob)
    term = tn(
        jnp.concatenate(split3(logit_part), axis=0).astype(BF16),
        jnp.concatenate([x_rows, x_rows, x_rows], axis=0),
    )[:experts]
    for part in range(experts):
        low = part * chunk
        high = min(width, low + chunk)
        if high <= low:
            term_s[part] = jnp.zeros((experts, chunk), F32)
            continue
        value = term[:, low:high]
        if high - low < chunk:
            value = jnp.concatenate([value, jnp.zeros((experts, chunk - high + low), F32)], axis=1)
        term_s[part] = value
    term_r[pl.ds(me, 1)] = term_s[pl.ds(me, 1)]
    scatter = exchange("expert", experts, me, lambda peer: term_s.at[peer], term_r.at[me], t_ss, t_rs)

    for tile in range(hidden // step_cols):
        cols = slice(tile * step_cols, (tile + 1) * step_cols)
        term = nt(pg_ref[:, cols], win[:, cols])
        if tile == 0:
            acc[...] = term
        else:
            acc[...] += term
    row_part = acc[...].reshape(groups, capacity, width)
    g1, g2, g3 = split3(gate_part)
    gate_tile = jnp.where(lane == 0, g1, jnp.where(lane == 1, g2, jnp.where(lane == 2, g3, 0.0)))
    right = [row_part[:, :, half:], gate_tile.reshape(groups, capacity, LANES)]
    if 2 * half > width + LANES:
        right.append(jnp.zeros((groups, capacity, 2 * half - width - LANES), F32))
    rows_s[...] = jnp.concatenate(
        [row_part[:, :, :half], jnp.concatenate(right, axis=2)], axis=1
    ).astype(BF16)
    rows_r[pl.ds(my_group, 1)] = rows_s[pl.ds(my_group, 1)]
    row_sum = exchange("dp", groups, my_group, lambda peer: rows_s.at[peer], rows_r.at[my_group], r_ss, r_rs)

    arrive(scatter)
    term_sum = term_r[0]
    for part in range(1, experts):
        term_sum = term_sum + term_r[part]
    sum_r[pl.ds(my_group, 1)] = term_sum[None]
    over_dp = exchange("dp", groups, my_group, lambda peer: sum_r.at[my_group], sum_r.at[my_group], s_ss, s_rs)

    arrive(row_sum)
    row_total = rows_r[0].astype(F32)
    for group in range(1, groups):
        row_total = row_total + rows_r[group].astype(F32)
    rest = width - half
    gate_lanes = row_total[capacity:, rest : rest + LANES]
    gate_total = jnp.sum(gate_lanes, axis=1, keepdims=True)
    row_grad = jnp.concatenate(
        [
            row_total[:capacity],
            row_total[capacity:, :rest],
            jnp.where(iota((capacity, LANES), 1) == me, gate_total, 0.0),
        ],
        axis=1,
    ).astype(BF16).astype(F32)
    returned = jnp.zeros((wide, back), F32)
    back_pieces = -(-(width + LANES) // back)
    for part in range(back_pieces):
        low = part * back
        high = min(width + LANES, low + back)
        give = jnp.where(from_owner & (row_u % SEG == SLOT * part + rank_row), 1.0, 0.0)
        term = nn(give, row_grad[:, low:high])
        if high - low < back:
            term = jnp.concatenate([term, jnp.zeros((wide, back - high + low), F32)], axis=1)
        returned = returned + term
    ret_s[...] = returned.astype(BF16).reshape(experts, SEG, back)
    ret_r[pl.ds(me, 1)] = ret_s[pl.ds(me, 1)]
    give_back = exchange("expert", experts, me, lambda peer: ret_s.at[peer], ret_r.at[me], b_ss, b_rs)

    arrive(over_dp)
    final = sum_r[0]
    for group in range(1, groups):
        final = final + sum_r[group]
    fin_r[pl.ds(me, 1)] = final[None]
    spread_out = exchange("expert", experts, me, lambda peer: fin_r.at[me], fin_r.at[me], f_ss, f_rs)

    marks = [
        jnp.where(seat_turned // SLOT == part, hit_turned, 0.0).astype(BF16)
        for part in range(back_pieces)
    ]
    r1, r2, r3 = split3(router)
    near = jnp.concatenate([r1, r2, r1, r3, r1, r2], axis=0).astype(BF16)

    arrive(give_back)
    ret_rows = ret_r[...].reshape(wide, back)
    gate_low = width - (back_pieces - 1) * back
    prob_grad = nt(
        ret_rows[:, gate_low : gate_low + LANES].T, marks[back_pieces - 1]
    )[:experts]
    logit_grad = prob * (prob_grad - jnp.sum(prob * prob_grad, axis=0, keepdims=True))
    l1, l2, l3 = split3(logit_grad)
    left = jnp.concatenate([l1, l1, l2, l1, l3, l2], axis=0).astype(BF16)
    gt_wide = tn(left, near)
    for part in range(back_pieces):
        low = part * back
        high = min(width, low + back)
        expert_sum = nn(marks[part], ret_rows[:, : high - low])
        gt_ref[:, low:high] = (expert_sum + gt_wide[:, low:high]).astype(BF16)

    stores[4].start()

    arrive(spread_out)
    for part in range(experts):
        low = part * chunk
        high = min(width, low + chunk)
        if high > low:
            gr_ref[:, low:high] = fin_r[part][:, : high - low]
    stores[5].start()
    for store in stores:
        store.wait()
    for copies in (dispatch, gather, row_sum, give_back, scatter, over_dp, spread_out):
        for copy in copies:
            copy.wait_send()


def weight_kernel(
    x_hbm, og_hbm, act_hbm, pg_hbm, gt_in, gr_in, gt_hbm, gin_hbm, gout_hbm, gr_hbm,
    x_ref, og_ref, act_ref, pg_ref, gin_ref, gout_ref, in_sem, out_sem,
):
    loads = []
    for source, target in (
        (x_hbm, x_ref), (pg_hbm, pg_ref), (act_hbm, act_ref), (og_hbm, og_ref), (gt_in, gt_hbm), (gr_in, gr_hbm)
    ):
        loads.append(pltpu.make_async_copy(source, target, in_sem.at[len(loads)]))
        loads[-1].start()
    stores = []

    def product(left, right, held, target):
        rows = held.shape[0]
        for low in range(0, rows, 256):
            span = slice(low, min(rows, low + 256))
            held[span, :] = tn(left[:, span], right[...]).astype(BF16)
            stores.append(pltpu.make_async_copy(held.at[span], target.at[0, span], out_sem.at[len(stores)]))
            stores[-1].start()

    loads[0].wait()
    loads[1].wait()
    product(x_ref, pg_ref, gin_ref, gin_hbm)
    loads[2].wait()
    loads[3].wait()
    product(act_ref, og_ref, gout_ref, gout_hbm)
    for copy in loads[4:] + stores:
        copy.wait()


def shards(experts, groups, tokens, cotangent, counts, picks, router, w_in, w_out):
    toks, width = tokens.shape
    capacity = picks.shape[2]
    hidden = w_in.shape[2]
    count = groups * capacity
    tiles = -(-width // LANES)
    pieces = SEG // (2 * SLOT)
    piece = LANES * -(-(tiles + 1) // pieces)
    whole = width + LANES
    half = LANES * -(-(tiles + 1) // 2)
    back = LANES * -(-(tiles + 1) // (SEG // SLOT))
    chunk = LANES * -(-tiles // experts)
    hbm = pl.BlockSpec(memory_space=pltpu.HBM)
    dma = pltpu.SemaphoreType.DMA
    over_e, over_g = dma((experts,)), dma((groups,))
    row_scratch = [
        pltpu.VMEM((count, width), BF16),
        pltpu.VMEM((count, width), BF16),
    ]
    results = pl.pallas_call(
        functools.partial(route_kernel, experts, groups),
        out_shape=(
            jax.ShapeDtypeStruct((count, width), BF16),
            jax.ShapeDtypeStruct((count, width), BF16),
            jax.ShapeDtypeStruct((count, hidden), BF16),
            jax.ShapeDtypeStruct((count, hidden), BF16),
            jax.ShapeDtypeStruct((toks, width), BF16),
            jax.ShapeDtypeStruct((experts, width), F32),
        ),
        in_specs=[hbm] * 7,
        out_specs=(hbm,) * 6,
        scratch_shapes=row_scratch
        + [
            pltpu.VMEM((toks, width), BF16),
            pltpu.VMEM((experts, width), F32),
            pltpu.VMEM((toks, width), BF16),
            pltpu.VMEM((toks, width), BF16),
            pltpu.VMEM((1, toks), jnp.int32),
            pltpu.VMEM((experts, capacity), jnp.int32),
            pltpu.VMEM((experts, width), F32),
            pltpu.VMEM((width, hidden), BF16),
            pltpu.VMEM((hidden, width), BF16),
            pltpu.VMEM((experts, SEG, piece), BF16),
            pltpu.VMEM((experts, SEG, piece), BF16),
            pltpu.VMEM((groups, 2 * capacity, whole), BF16),
            pltpu.VMEM((count, hidden), BF16),
            pltpu.VMEM((count, hidden), BF16),
            pltpu.VMEM((count, width), F32),
            pltpu.VMEM((groups, 2 * capacity, half), BF16),
            pltpu.VMEM((groups, 2 * capacity, half), BF16),
            pltpu.VMEM((experts, SEG, back), BF16),
            pltpu.VMEM((experts, SEG, back), BF16),
            pltpu.VMEM((experts, experts, chunk), F32),
            pltpu.VMEM((experts, experts, chunk), F32),
            pltpu.VMEM((groups, experts, chunk), F32),
            pltpu.VMEM((experts, experts, chunk), F32),
            dma((7,)),
            dma((6,)),
            over_e, over_e,
            over_g, over_g,
            over_g, over_g,
            over_e, over_e,
            over_e, over_e,
            over_g, over_g,
            over_e, over_e,
        ],
        compiler_params=pltpu.CompilerParams(
            collective_id=0, has_side_effects=True, vmem_limit_bytes=58 * 1024 * 1024
        ),
        name="route",
    )(tokens, cotangent, counts.reshape(1, toks), picks[0], router.T, w_in[0], w_out[0])

    grad_tokens, grad_in, grad_out, grad_router = pl.pallas_call(
        weight_kernel,
        out_shape=(
            jax.ShapeDtypeStruct((toks, width), BF16),
            jax.ShapeDtypeStruct((1, width, hidden), BF16),
            jax.ShapeDtypeStruct((1, hidden, width), BF16),
            jax.ShapeDtypeStruct((experts, width), F32),
        ),
        in_specs=[hbm] * 6,
        out_specs=(hbm,) * 4,
        scratch_shapes=row_scratch
        + [
            pltpu.VMEM((count, hidden), BF16),
            pltpu.VMEM((count, hidden), BF16),
            pltpu.VMEM((width, hidden), BF16),
            pltpu.VMEM((hidden, width), BF16),
            dma((6,)),
            dma((-(-width // 256) + -(-hidden // 256),)),
        ],
        compiler_params=pltpu.CompilerParams(vmem_limit_bytes=58 * 1024 * 1024),
        name="weight_grads",
    )(*results)
    return grad_tokens, grad_in, grad_out, grad_router.T


def solution(mesh):
    placed = (
        P(("dp", "expert"), None),
        P(("dp", "expert"), None),
        P(("dp", "expert")),
        P("dp", None, None),
        P(),
        P("expert", None, "dp"),
        P("expert", "dp", None),
    )
    return jax.shard_map(
        functools.partial(shards, mesh.shape["expert"], mesh.shape["dp"]),
        mesh=mesh,
        in_specs=placed,
        out_specs=(
            P(("dp", "expert"), None),
            P("expert", None, "dp"),
            P("expert", "dp", None),
            P(),
        ),
        check_vma=False,
    )
```

time: 48.6 us -> 46.7 us (0.961)
  local copies, waits for them, and re-layouts: 7.5 us -> 0 us
  Pallas kernels: 40.1 us -> 45.9 us
    pallas_call x1, Pallas kernels: 4.33 us -> 15.8 us  [shards(): pl.pallas_call(weight_kernel, out_shape=(jax.ShapeDtypeStruct((toks, widt...]
    unnamed x14 -> x0, local copies, waits for them, and re-layouts: 7.5 us -> none
    pallas_call x1, Pallas kernels: 35.7 us -> 30.1 us  [shards(): pl.pallas_call(functools.partial(route_kernel, experts, groups), out_shap...]
where the time goes in v2:
time: 46.7 us; the launch traced here: 46.5 us
  Pallas kernels  45.9 us (98%)
  between operations  0.64 us (1%)
    pallas_call x1, Pallas kernels, shards(): pl.pallas_call(functools.partial(route_kernel, experts, groups), out_shap...  30.1 us
    pallas_call x1, Pallas kernels, shards(): pl.pallas_call(weight_kernel, out_shape=(jax.ShapeDtypeStruct((toks, widt...  15.8 us

profile of v2, /device:TPU:0, one launch (start us, length us, event | category | flops | bytes accessed | tf_op | source)
XLA Modules:
  0.0 46.5 jit_solution(15325777503640495424)
XLA Ops:
  0.6 30.1 %route.1 = (bf16[32,1664]{1,0:T(8,128)(2,1)}, bf16[32,1664]{1,0:T(8,128)(2,1)}, bf16[32,1024]{1,0:T(8,128)(2,1)}, bf16[32,1024]{1,0:T(8,128)(2,1)}, bf16[128,1664]{1,0:T(8,128)(2,1)}, /*index=5*/f32[8,1664]{1,0:T(8,128)}) custom-call(bf16[128,1664]{1,0:T(8,128)(2,1)} %tok_hbm.1, bf16[128,1664]{1,0:T(8,128)(2,1)} %cot_hbm.1, s32[1,128]{1,0:T(1,128)} %bitcast.10, ...), custom_call_target="tpu_custom_call" | custom-call | tf_op jit(solution)/shard_map/route/pallas_call | solution.py:410
  30.7 15.8 %weight_grads.1 = (bf16[128,1664]{1,0:T(8,128)(2,1)}, bf16[1,1664,1024]{2,1,0:T(8,128)(2,1)}, bf16[1,1024,1664]{2,1,0:T(8,128)(2,1)}, f32[8,1664]{1,0:T(8,128)}) custom-call(bf16[32,1664]{1,0:T(8,128)(2,1)} %get-tuple-element.14.x_hbm, bf16[32,1664]{1,0:T(8,128)(2,1)} %get-tuple-element.15.og_hbm, bf16[32,1024]{1,0:T(8,128)(2,1)} %get-tuple-element.16.act_hbm, ...), custom_call_target="tpu_custom_call" | custom-call | tf_op jit(solution)/shard_map/weight_grads/pallas_call | solution.py:463

commit v3 on v2

--- a/solution.py
+++ b/solution.py
@@ -72,9 +72,9 @@
     experts, groups, tok_hbm, cot_hbm, cnt_hbm, pick_hbm, router_hbm, win_hbm, wout_hbm,
     x_hbm, og_hbm, act_hbm, pg_hbm, gt_hbm, gr_hbm,
     x_ref, og_ref, gt_ref, gr_ref, tok_ref, cot_ref, cnt_ref, pick_ref, router_ref, win, wout,
-    send, recv, pack, act_ref, pg_ref, acc, rows_s, rows_r, ret_s, ret_r,
+    send, recv, pack_x, pack_d, act_ref, pg_ref, slope_ref, head_s, head_r, tail_s, tail_r, ret_s, ret_r,
     term_s, term_r, sum_r, fin_r,
-    in_sem, out_sem, d_ss, d_rs, p_ss, p_rs, r_ss, r_rs, b_ss, b_rs, t_ss, t_rs, s_ss, s_rs, f_ss, f_rs,
+    in_sem, out_sem, d_ss, d_rs, x_ss, x_rs, y_ss, y_rs, h_ss, h_rs, r_ss, r_rs, b_ss, b_rs, t_ss, t_rs, s_ss, s_rs, f_ss, f_rs,
 ):
     me = lax.axis_index("expert")
     my_group = lax.axis_index("dp")
@@ -83,7 +83,9 @@
     hidden = win.shape[1]
     count = groups * capacity
     piece = send.shape[2]
-    half = rows_s.shape[2]
+    half = pack_x.shape[2]
+    whole = 2 * half
+    head = 2 * head_s.shape[2]
     back = ret_s.shape[2]
     chunk = term_s.shape[2]
 
@@ -196,44 +198,59 @@
 
     arrive(dispatch)
     rows_in = recv[...].reshape(wide, piece)
-    whole = pack.shape[2]
+    packed = []
     for part in range(pieces):
-        low = part * piece
-        high = min(whole, low + piece)
-        packed = nn(blocks[part], rows_in[:, : high - low]).astype(BF16)
-        pack[pl.ds(my_group, 1), :, low:high] = packed[None]
-    gather = exchange("dp", groups, my_group, lambda peer: pack.at[my_group], pack.at[my_group], p_ss, p_rs)
+        taken = min(whole, (part + 1) * piece) - part * piece
+        packed.append(nn(blocks[part], rows_in[:, :taken]))
+    packed = jnp.concatenate(packed, axis=1)
+
+    def folded(rows):
+        return jnp.concatenate([rows[..., :half], rows[..., half:]], axis=-2).astype(BF16)
+
+    def unfolded(pack):
+        rows = pack[...].astype(F32)
+        return jnp.concatenate([rows[:, :capacity], rows[:, capacity:]], axis=2).reshape(count, whole)
+
+    pack_x[pl.ds(my_group, 1)] = folded(packed[:capacity])[None]
+    gather_x = exchange(
+        "dp", groups, my_group, lambda peer: pack_x.at[my_group], pack_x.at[my_group], x_ss, x_rs
+    )
+    pack_d[pl.ds(my_group, 1)] = folded(packed[capacity:])[None]
+    gather_d = exchange(
+        "dp", groups, my_group, lambda peer: pack_d.at[my_group], pack_d.at[my_group], y_ss, y_rs
+    )
     load_in.wait()
     load_out.wait()
-    arrive(gather)
-
-    every = pack[...].astype(F32)
-    x_rows = every[:, :capacity, :width].reshape(count, width).astype(BF16)
-    dy_wide = every[:, capacity:, :width].reshape(count, width)
-    gate_lanes = every[:, capacity:, width : width + LANES].reshape(count, LANES)
+    arrive(gather_x)
+
+    x_rows = unfolded(pack_x)[:, :width].astype(BF16)
+    x_ref[...] = x_rows
+    stores[0].start()
+    step_cols = min(hidden, 256)
+    for tile in range(hidden // step_cols):
+        cols = slice(tile * step_cols, (tile + 1) * step_cols)
+        pre = nn(x_rows, win[:, cols])
+        cdf = normal_cdf(pre)
+        act_ref[:, cols] = (pre * cdf).astype(BF16)
+        slope_ref[:, cols] = cdf + pre * jnp.exp(-0.5 * pre * pre) * 0.3989422804014327
+    stores[2].start()
+
+    arrive(gather_d)
+    dy_full = unfolded(pack_d)
+    dy_wide = dy_full[:, :width]
+    gate_lanes = dy_full[:, width : width + LANES]
     lane = iota((count, LANES), 1)
     gate = jnp.sum(jnp.where(lane == me, gate_lanes, 0.0), axis=1, keepdims=True)
     dy_rows = dy_wide.astype(BF16)
-    x_ref[...] = x_rows
-    og_ref[...] = (gate * dy_wide).astype(BF16)
-    stores[0].start()
-    stores[1].start()
-
-    step_cols = min(hidden, 256)
     gate_part = jnp.zeros((count, 1), F32)
     for tile in range(hidden // step_cols):
         cols = slice(tile * step_cols, (tile + 1) * step_cols)
-        pre = nn(x_rows, win[:, cols])
         back_act = nt(dy_rows, wout[cols, :])
-        cdf = normal_cdf(pre)
-        act = (pre * cdf).astype(BF16)
-        slope = cdf + pre * jnp.exp(-0.5 * pre * pre) * 0.3989422804014327
-        act_ref[:, cols] = act
-        pg_ref[:, cols] = (gate * back_act * slope).astype(BF16)
-        gate_part = gate_part + jnp.sum(act.astype(F32) * back_act, axis=1, keepdims=True)
-
-    stores[2].start()
+        pg_ref[:, cols] = (gate * back_act * slope_ref[:, cols]).astype(BF16)
+        gate_part = gate_part + jnp.sum(act_ref[:, cols].astype(F32) * back_act, axis=1, keepdims=True)
     stores[3].start()
+    og_ref[...] = (gate * dy_wide).astype(BF16)
+    stores[1].start()
 
     fold_row, fold_col = iota((LANES, LANES), 0), iota((LANES, LANES), 1)
     fold = one_hot((fold_row % experts == fold_col) & (fold_row < 3 * experts))
@@ -257,24 +274,30 @@
     term_r[pl.ds(me, 1)] = term_s[pl.ds(me, 1)]
     scatter = exchange("expert", experts, me, lambda peer: term_s.at[peer], term_r.at[me], t_ss, t_rs)
 
-    for tile in range(hidden // step_cols):
-        cols = slice(tile * step_cols, (tile + 1) * step_cols)
-        term = nt(pg_ref[:, cols], win[:, cols])
-        if tile == 0:
-            acc[...] = term
-        else:
-            acc[...] += term
-    row_part = acc[...].reshape(groups, capacity, width)
+    pre_grad = pg_ref[...]
+
+    def row_columns(low, high):
+        return [
+            nt(pre_grad, win[start : min(high, start + 256), :]) for start in range(low, high, 256)
+        ]
+
+    def to_groups(columns, sent, kept, send_sem, recv_sem):
+        rows = jnp.concatenate(columns, axis=1).reshape(groups, capacity, 2 * sent.shape[2])
+        side = sent.shape[2]
+        sent[...] = jnp.concatenate([rows[:, :, :side], rows[:, :, side:]], axis=1).astype(BF16)
+        kept[pl.ds(my_group, 1)] = sent[pl.ds(my_group, 1)]
+        return exchange(
+            "dp", groups, my_group, lambda peer: sent.at[peer], kept.at[my_group], send_sem, recv_sem
+        )
+
+    head_sum = to_groups(row_columns(0, head), head_s, head_r, h_ss, h_rs)
     g1, g2, g3 = split3(gate_part)
-    gate_tile = jnp.where(lane == 0, g1, jnp.where(lane == 1, g2, jnp.where(lane == 2, g3, 0.0)))
-    right = [row_part[:, :, half:], gate_tile.reshape(groups, capacity, LANES)]
-    if 2 * half > width + LANES:
-        right.append(jnp.zeros((groups, capacity, 2 * half - width - LANES), F32))
-    rows_s[...] = jnp.concatenate(
-        [row_part[:, :, :half], jnp.concatenate(right, axis=2)], axis=1
-    ).astype(BF16)
-    rows_r[pl.ds(my_group, 1)] = rows_s[pl.ds(my_group, 1)]
-    row_sum = exchange("dp", groups, my_group, lambda peer: rows_s.at[peer], rows_r.at[my_group], r_ss, r_rs)
+    tail = row_columns(head, width)
+    tail.append(jnp.where(lane == 0, g1, jnp.where(lane == 1, g2, jnp.where(lane == 2, g3, 0.0))))
+    spare = head + 2 * tail_s.shape[2] - width - LANES
+    if spare:
+        tail.append(jnp.zeros((count, spare), F32))
+    tail_sum = to_groups(tail, tail_s, tail_r, r_ss, r_rs)
 
     arrive(scatter)
     term_sum = term_r[0]
@@ -283,17 +306,20 @@
     sum_r[pl.ds(my_group, 1)] = term_sum[None]
     over_dp = exchange("dp", groups, my_group, lambda peer: sum_r.at[my_group], sum_r.at[my_group], s_ss, s_rs)
 
-    arrive(row_sum)
-    row_total = rows_r[0].astype(F32)
-    for group in range(1, groups):
-        row_total = row_total + rows_r[group].astype(F32)
-    rest = width - half
-    gate_lanes = row_total[capacity:, rest : rest + LANES]
-    gate_total = jnp.sum(gate_lanes, axis=1, keepdims=True)
+    def over_blocks(kept):
+        summed = kept[0].astype(F32)
+        for group in range(1, groups):
+            summed = summed + kept[group].astype(F32)
+        return [summed[:capacity], summed[capacity:]]
+
+    arrive(head_sum)
+    row_sides = over_blocks(head_r)
+    arrive(tail_sum)
+    row_total = jnp.concatenate(row_sides + over_blocks(tail_r), axis=1)
+    gate_total = jnp.sum(row_total[:, width : width + LANES], axis=1, keepdims=True)
     row_grad = jnp.concatenate(
         [
-            row_total[:capacity],
-            row_total[capacity:, :rest],
+            row_total[:, :width],
             jnp.where(iota((capacity, LANES), 1) == me, gate_total, 0.0),
         ],
         axis=1,
@@ -353,18 +379,18 @@
     stores[5].start()
     for store in stores:
         store.wait()
-    for copies in (dispatch, gather, row_sum, give_back, scatter, over_dp, spread_out):
+    for copies in (dispatch, gather_x, gather_d, head_sum, tail_sum, give_back, scatter, over_dp, spread_out):
         for copy in copies:
             copy.wait_send()
 
 
 def weight_kernel(
     x_hbm, og_hbm, act_hbm, pg_hbm, gt_in, gr_in, gt_hbm, gin_hbm, gout_hbm, gr_hbm,
-    x_ref, og_ref, act_ref, pg_ref, gin_ref, gout_ref, in_sem, out_sem,
+    x_ref, og_ref, act_ref, pg_ref, gt_ref, gr_ref, gin_ref, gout_ref, in_sem, out_sem,
 ):
     loads = []
     for source, target in (
-        (x_hbm, x_ref), (pg_hbm, pg_ref), (act_hbm, act_ref), (og_hbm, og_ref), (gt_in, gt_hbm), (gr_in, gr_hbm)
+        (x_hbm, x_ref), (pg_hbm, pg_ref), (act_hbm, act_ref), (og_hbm, og_ref), (gt_in, gt_ref), (gr_in, gr_ref)
     ):
         loads.append(pltpu.make_async_copy(source, target, in_sem.at[len(loads)]))
         loads[-1].start()
@@ -381,11 +407,15 @@
     loads[0].wait()
     loads[1].wait()
     product(x_ref, pg_ref, gin_ref, gin_hbm)
+    for load, held, target in ((loads[4], gt_ref, gt_hbm), (loads[5], gr_ref, gr_hbm)):
+        load.wait()
+        stores.append(pltpu.make_async_copy(held, target, out_sem.at[len(stores)]))
+        stores[-1].start()
     loads[2].wait()
     loads[3].wait()
     product(act_ref, og_ref, gout_ref, gout_hbm)
-    for copy in loads[4:] + stores:
-        copy.wait()
+    for store in stores:
+        store.wait()
 
 
 def shards(experts, groups, tokens, cotangent, counts, picks, router, w_in, w_out):
@@ -396,9 +426,10 @@
     tiles = -(-width // LANES)
     pieces = SEG // (2 * SLOT)
     piece = LANES * -(-(tiles + 1) // pieces)
-    whole = width + LANES
     half = LANES * -(-(tiles + 1) // 2)
     back = LANES * -(-(tiles + 1) // (SEG // SLOT))
+    head = LANES * ((tiles + 1) * 2 // 7)
+    tail = half - head
     chunk = LANES * -(-tiles // experts)
     hbm = pl.BlockSpec(memory_space=pltpu.HBM)
     dma = pltpu.SemaphoreType.DMA
@@ -432,12 +463,15 @@
             pltpu.VMEM((hidden, width), BF16),
             pltpu.VMEM((experts, SEG, piece), BF16),
             pltpu.VMEM((experts, SEG, piece), BF16),
-            pltpu.VMEM((groups, 2 * capacity, whole), BF16),
+            pltpu.VMEM((groups, 2 * capacity, half), BF16),
+            pltpu.VMEM((groups, 2 * capacity, half), BF16),
             pltpu.VMEM((count, hidden), BF16),
             pltpu.VMEM((count, hidden), BF16),
-            pltpu.VMEM((count, width), F32),
-            pltpu.VMEM((groups, 2 * capacity, half), BF16),
-            pltpu.VMEM((groups, 2 * capacity, half), BF16),
+            pltpu.VMEM((count, hidden), F32),
+            pltpu.VMEM((groups, 2 * capacity, head), BF16),
+            pltpu.VMEM((groups, 2 * capacity, head), BF16),
+            pltpu.VMEM((groups, 2 * capacity, tail), BF16),
+            pltpu.VMEM((groups, 2 * capacity, tail), BF16),
             pltpu.VMEM((experts, SEG, back), BF16),
             pltpu.VMEM((experts, SEG, back), BF16),
             pltpu.VMEM((experts, experts, chunk), F32),
@@ -447,6 +481,8 @@
             dma((7,)),
             dma((6,)),
             over_e, over_e,
+            over_g, over_g,
+            over_g, over_g,
             over_g, over_g,
             over_g, over_g,
             over_e, over_e,
@@ -474,10 +510,12 @@
         + [
             pltpu.VMEM((count, hidden), BF16),
             pltpu.VMEM((count, hidden), BF16),
+            pltpu.VMEM((toks, width), BF16),
+            pltpu.VMEM((experts, width), F32),
             pltpu.VMEM((width, hidden), BF16),
             pltpu.VMEM((hidden, width), BF16),
             dma((6,)),
-            dma((-(-width // 256) + -(-hidden // 256),)),
+            dma((-(-width // 256) + -(-hidden // 256) + 2,)),
         ],
         compiler_params=pltpu.CompilerParams(vmem_limit_bytes=58 * 1024 * 1024),
         name="weight_grads",

time: 46.7 us -> 34.8 us (0.75)
  Pallas kernels: 45.9 us -> 34 us
    pallas_call x1, Pallas kernels: 15.8 us -> 4.35 us  [shards(): pl.pallas_call(weight_kernel, out_shape=(jax.ShapeDtypeStruct((toks, widt...]
where the time goes in v3:
time: 34.8 us; the launch traced here: 34.6 us
  Pallas kernels  34 us (98%)
  between operations  0.64 us (2%)
    pallas_call x1, Pallas kernels, shards(): pl.pallas_call(functools.partial(route_kernel, experts, groups), out_shap...  29.6 us
    pallas_call x1, Pallas kernels, shards(): pl.pallas_call(weight_kernel, out_shape=(jax.ShapeDtypeStruct((toks, widt...  4.35 us

profile of v3, /device:TPU:0, one launch (start us, length us, event | category | flops | bytes accessed | tf_op | source)
XLA Modules:
  0.0 34.6 jit_solution(4138295539573897205)
XLA Ops:
  0.6 29.6 %route.1 = (bf16[32,1664]{1,0:T(8,128)(2,1)}, bf16[32,1664]{1,0:T(8,128)(2,1)}, bf16[32,1024]{1,0:T(8,128)(2,1)}, bf16[32,1024]{1,0:T(8,128)(2,1)}, bf16[128,1664]{1,0:T(8,128)(2,1)}, /*index=5*/f32[8,1664]{1,0:T(8,128)}) custom-call(bf16[128,1664]{1,0:T(8,128)(2,1)} %tok_hbm.1, bf16[128,1664]{1,0:T(8,128)(2,1)} %cot_hbm.1, s32[1,128]{1,0:T(1,128)} %bitcast.10, ...), custom_call_target="tpu_custom_call" | custom-call | tf_op jit(solution)/shard_map/route/pallas_call | solution.py:441
  30.3 4.4 %weight_grads.1 = (bf16[128,1664]{1,0:T(8,128)(2,1)}, bf16[1,1664,1024]{2,1,0:T(8,128)(2,1)}, bf16[1,1024,1664]{2,1,0:T(8,128)(2,1)}, f32[8,1664]{1,0:T(8,128)}) custom-call(bf16[32,1664]{1,0:T(8,128)(2,1)} %get-tuple-element.14.x_hbm, bf16[32,1664]{1,0:T(8,128)(2,1)} %get-tuple-element.15.og_hbm, bf16[32,1024]{1,0:T(8,128)(2,1)} %get-tuple-element.16.act_hbm, ...), custom_call_target="tpu_custom_call" | custom-call | tf_op jit(solution)/shard_map/weight_grads/pallas_call | solution.py:499

commit v4 on v3

--- a/solution.py
+++ b/solution.py
@@ -72,9 +72,9 @@
     experts, groups, tok_hbm, cot_hbm, cnt_hbm, pick_hbm, router_hbm, win_hbm, wout_hbm,
     x_hbm, og_hbm, act_hbm, pg_hbm, gt_hbm, gr_hbm,
     x_ref, og_ref, gt_ref, gr_ref, tok_ref, cot_ref, cnt_ref, pick_ref, router_ref, win, wout,
-    send, recv, pack_x, pack_d, act_ref, pg_ref, slope_ref, head_s, head_r, tail_s, tail_r, ret_s, ret_r,
+    send, recv, gate_s, gate_r, pack_x, pack_d, act_ref, pg_ref, slope_ref, head_s, head_r, tail_s, tail_r, ret_s, ret_r,
     term_s, term_r, sum_r, fin_r,
-    in_sem, out_sem, d_ss, d_rs, x_ss, x_rs, y_ss, y_rs, h_ss, h_rs, r_ss, r_rs, b_ss, b_rs, t_ss, t_rs, s_ss, s_rs, f_ss, f_rs,
+    in_sem, out_sem, d_ss, d_rs, g_ss, g_rs, x_ss, x_rs, y_ss, y_rs, h_ss, h_rs, r_ss, r_rs, b_ss, b_rs, t_ss, t_rs, s_ss, s_rs, f_ss, f_rs,
 ):
     me = lax.axis_index("expert")
     my_group = lax.axis_index("dp")
@@ -134,11 +134,7 @@
     part_of = iota((wide, 2 * toks), 0) % SEG // (2 * SLOT)
 
     load_tok.wait()
-    load_router.wait()
     tok = tok_ref[...]
-    router = router_ref[...]
-    stacked = jnp.concatenate(split3(router), axis=0).astype(BF16)
-    parts = nt(stacked, tok)
     load_cnt.wait()
     load_cot.wait()
     load_in.start()
@@ -146,10 +142,7 @@
     weight_row = jnp.maximum(cnt_ref[...], 1).astype(F32)
     diagonal = iota((toks, toks), 0) == iota((toks, toks), 1)
     weight = jnp.sum(jnp.where(diagonal, weight_row, 0.0), axis=1, keepdims=True)
-    scaled = (cot_ref[...].astype(F32) / weight).astype(BF16)
-    logits = parts[:experts] + parts[experts : 2 * experts] + parts[2 * experts :]
-    raised = jnp.exp(logits - jnp.max(logits, axis=0, keepdims=True))
-    prob = raised / jnp.sum(raised, axis=0, keepdims=True)
+    scaled = (cot_ref[...].astype(F32) * (1.0 / weight)).astype(BF16)
 
     pieces = SEG // (2 * SLOT)
     both = jnp.concatenate([tok, scaled], axis=0)
@@ -159,21 +152,28 @@
         high = min(width, low + piece)
         chosen = jnp.where(part_of == part, take, 0.0).astype(BF16)
         term = nn(chosen, both[:, low:high])
-        if part == pieces - 1:
-            padded = jnp.concatenate(
-                split3(prob) + (jnp.zeros((LANES - 3 * experts, toks), F32),), axis=0
-            )
-            columns = [term, nt(chosen[:, toks:], padded.astype(BF16))]
-            spare = piece - (high - low) - LANES
-            if spare:
-                columns.append(jnp.zeros((wide, spare), F32))
-            term = jnp.concatenate(columns, axis=1)
+        if high - low < piece:
+            term = jnp.concatenate([term, jnp.zeros((wide, piece - high + low), F32)], axis=1)
         total = total + term
     send[...] = total.astype(BF16).reshape(experts, SEG, piece)
     recv[pl.ds(me, 1)] = send[pl.ds(me, 1)]
 
     pl.semaphore_wait(barrier, experts - 1 + groups - 1)
     dispatch = exchange("expert", experts, me, lambda peer: send.at[peer], recv.at[me], d_ss, d_rs)
+
+    load_router.wait()
+    router = router_ref[...]
+    stacked = jnp.concatenate(split3(router), axis=0).astype(BF16)
+    parts = nt(stacked, tok)
+    logits = parts[:experts] + parts[experts : 2 * experts] + parts[2 * experts :]
+    raised = jnp.exp(logits - jnp.max(logits, axis=0, keepdims=True))
+    prob = raised / jnp.sum(raised, axis=0, keepdims=True)
+    padded = jnp.concatenate(
+        split3(prob) + (jnp.zeros((LANES - 3 * experts, toks), F32),), axis=0
+    )
+    gate_s[...] = nt(hit.astype(BF16), padded.astype(BF16)).astype(BF16).reshape(experts, SEG, LANES)
+    gate_r[pl.ds(me, 1)] = gate_s[pl.ds(me, 1)]
+    send_gates = exchange("expert", experts, me, lambda peer: gate_s.at[peer], gate_r.at[me], g_ss, g_rs)
 
     mine = iota((experts, capacity), 0) == me
     owner_row = jnp.sum(jnp.where(mine, owner, 0), axis=0, keepdims=True)
@@ -189,6 +189,10 @@
         seat_c % (2 * SLOT) == SLOT * is_dy + rank_col
     )
     blocks = [one_hot(wanted & (seat_c // (2 * SLOT) == part)) for part in range(pieces)]
+    gate_block = one_hot(
+        (iota((capacity, wide), 1) // SEG == owner_col[:capacity])
+        & (iota((capacity, wide), 1) % SEG == rank_col[:capacity])
+    )
     before = same[:capacity] & (slot_row[:capacity] < slot_col[:capacity])
     rank_row = jnp.sum(jnp.where(before, 1, 0), axis=0, keepdims=True)
     row_u = iota((wide, capacity), 0)
@@ -200,8 +204,9 @@
     rows_in = recv[...].reshape(wide, piece)
     packed = []
     for part in range(pieces):
-        taken = min(whole, (part + 1) * piece) - part * piece
+        taken = min(width, (part + 1) * piece) - part * piece
         packed.append(nn(blocks[part], rows_in[:, :taken]))
+    packed.append(jnp.zeros((tall, whole - width), F32))
     packed = jnp.concatenate(packed, axis=1)
 
     def folded(rows):
@@ -215,7 +220,12 @@
     gather_x = exchange(
         "dp", groups, my_group, lambda peer: pack_x.at[my_group], pack_x.at[my_group], x_ss, x_rs
     )
-    pack_d[pl.ds(my_group, 1)] = folded(packed[capacity:])[None]
+    arrive(send_gates)
+    gate_rows = nn(gate_block, gate_r[...].reshape(wide, LANES))
+    packed_d = [packed[capacity:, :width], gate_rows]
+    if whole > width + LANES:
+        packed_d.append(jnp.zeros((capacity, whole - width - LANES), F32))
+    pack_d[pl.ds(my_group, 1)] = folded(jnp.concatenate(packed_d, axis=1))[None]
     gather_d = exchange(
         "dp", groups, my_group, lambda peer: pack_d.at[my_group], pack_d.at[my_group], y_ss, y_rs
     )
@@ -251,6 +261,31 @@
     stores[3].start()
     og_ref[...] = (gate * dy_wide).astype(BF16)
     stores[1].start()
+
+    pre_grad = pg_ref[...]
+
+    def row_columns(low, high):
+        return [
+            nt(pre_grad, win[start : min(high, start + 256), :]) for start in range(low, high, 256)
+        ]
+
+    def to_groups(columns, sent, kept, send_sem, recv_sem):
+        rows = jnp.concatenate(columns, axis=1).reshape(groups, capacity, 2 * sent.shape[2])
+        side = sent.shape[2]
+        sent[...] = jnp.concatenate([rows[:, :, :side], rows[:, :, side:]], axis=1).astype(BF16)
+        kept[pl.ds(my_group, 1)] = sent[pl.ds(my_group, 1)]
+        return exchange(
+            "dp", groups, my_group, lambda peer: sent.at[peer], kept.at[my_group], send_sem, recv_sem
+        )
+
+    head_sum = to_groups(row_columns(0, head), head_s, head_r, h_ss, h_rs)
+    g1, g2, g3 = split3(gate_part)
+    tail = row_columns(head, width)
+    tail.append(jnp.where(lane == 0, g1, jnp.where(lane == 1, g2, jnp.where(lane == 2, g3, 0.0))))
+    spare = head + 2 * tail_s.shape[2] - width - LANES
+    if spare:
+        tail.append(jnp.zeros((count, spare), F32))
+    tail_sum = to_groups(tail, tail_s, tail_r, r_ss, r_rs)
 
     fold_row, fold_col = iota((LANES, LANES), 0), iota((LANES, LANES), 1)
     fold = one_hot((fold_row % experts == fold_col) & (fold_row < 3 * experts))
@@ -273,38 +308,6 @@
         term_s[part] = value
     term_r[pl.ds(me, 1)] = term_s[pl.ds(me, 1)]
     scatter = exchange("expert", experts, me, lambda peer: term_s.at[peer], term_r.at[me], t_ss, t_rs)
-
-    pre_grad = pg_ref[...]
-
-    def row_columns(low, high):
-        return [
-            nt(pre_grad, win[start : min(high, start + 256), :]) for start in range(low, high, 256)
-        ]
-
-    def to_groups(columns, sent, kept, send_sem, recv_sem):
-        rows = jnp.concatenate(columns, axis=1).reshape(groups, capacity, 2 * sent.shape[2])
-        side = sent.shape[2]
-        sent[...] = jnp.concatenate([rows[:, :, :side], rows[:, :, side:]], axis=1).astype(BF16)
-        kept[pl.ds(my_group, 1)] = sent[pl.ds(my_group, 1)]
-        return exchange(
-            "dp", groups, my_group, lambda peer: sent.at[peer], kept.at[my_group], send_sem, recv_sem
-        )
-
-    head_sum = to_groups(row_columns(0, head), head_s, head_r, h_ss, h_rs)
-    g1, g2, g3 = split3(gate_part)
-    tail = row_columns(head, width)
-    tail.append(jnp.where(lane == 0, g1, jnp.where(lane == 1, g2, jnp.where(lane == 2, g3, 0.0))))
-    spare = head + 2 * tail_s.shape[2] - width - LANES
-    if spare:
-        tail.append(jnp.zeros((count, spare), F32))
-    tail_sum = to_groups(tail, tail_s, tail_r, r_ss, r_rs)
-
-    arrive(scatter)
-    term_sum = term_r[0]
-    for part in range(1, experts):
-        term_sum = term_sum + term_r[part]
-    sum_r[pl.ds(my_group, 1)] = term_sum[None]
-    over_dp = exchange("dp", groups, my_group, lambda peer: sum_r.at[my_group], sum_r.at[my_group], s_ss, s_rs)
 
     def over_blocks(kept):
         summed = kept[0].astype(F32)
@@ -338,19 +341,26 @@
     ret_r[pl.ds(me, 1)] = ret_s[pl.ds(me, 1)]
     give_back = exchange("expert", experts, me, lambda peer: ret_s.at[peer], ret_r.at[me], b_ss, b_rs)
 
+    arrive(scatter)
+    term_sum = term_r[0]
+    for part in range(1, experts):
+        term_sum = term_sum + term_r[part]
+    sum_r[pl.ds(my_group, 1)] = term_sum[None]
+    over_dp = exchange("dp", groups, my_group, lambda peer: sum_r.at[my_group], sum_r.at[my_group], s_ss, s_rs)
+
+    marks = [
+        jnp.where(seat_turned // SLOT == part, hit_turned, 0.0).astype(BF16)
+        for part in range(back_pieces)
+    ]
+    r1, r2, r3 = split3(router)
+    near = jnp.concatenate([r1, r2, r1, r3, r1, r2], axis=0).astype(BF16)
+
     arrive(over_dp)
     final = sum_r[0]
     for group in range(1, groups):
         final = final + sum_r[group]
     fin_r[pl.ds(me, 1)] = final[None]
     spread_out = exchange("expert", experts, me, lambda peer: fin_r.at[me], fin_r.at[me], f_ss, f_rs)
-
-    marks = [
-        jnp.where(seat_turned // SLOT == part, hit_turned, 0.0).astype(BF16)
-        for part in range(back_pieces)
-    ]
-    r1, r2, r3 = split3(router)
-    near = jnp.concatenate([r1, r2, r1, r3, r1, r2], axis=0).astype(BF16)
 
     arrive(give_back)
     ret_rows = ret_r[...].reshape(wide, back)
@@ -379,7 +389,7 @@
     stores[5].start()
     for store in stores:
         store.wait()
-    for copies in (dispatch, gather_x, gather_d, head_sum, tail_sum, give_back, scatter, over_dp, spread_out):
+    for copies in (dispatch, send_gates, gather_x, gather_d, head_sum, tail_sum, give_back, scatter, over_dp, spread_out):
         for copy in copies:
             copy.wait_send()
 
@@ -425,7 +435,7 @@
     count = groups * capacity
     tiles = -(-width // LANES)
     pieces = SEG // (2 * SLOT)
-    piece = LANES * -(-(tiles + 1) // pieces)
+    piece = LANES * -(-tiles // pieces)
     half = LANES * -(-(tiles + 1) // 2)
     back = LANES * -(-(tiles + 1) // (SEG // SLOT))
     head = LANES * ((tiles + 1) * 2 // 7)
@@ -463,6 +473,8 @@
             pltpu.VMEM((hidden, width), BF16),
             pltpu.VMEM((experts, SEG, piece), BF16),
             pltpu.VMEM((experts, SEG, piece), BF16),
+            pltpu.VMEM((experts, SEG, LANES), BF16),
+            pltpu.VMEM((experts, SEG, LANES), BF16),
             pltpu.VMEM((groups, 2 * capacity, half), BF16),
             pltpu.VMEM((groups, 2 * capacity, half), BF16),
             pltpu.VMEM((count, hidden), BF16),
@@ -480,6 +492,7 @@
             pltpu.VMEM((experts, experts, chunk), F32),
             dma((7,)),
             dma((6,)),
+            over_e, over_e,
             over_e, over_e,
             over_g, over_g,
             over_g, over_g,

time: 34.8 us -> 36.4 us (1.046)
  Pallas kernels: 34 us -> 35.6 us
    pallas_call x1, Pallas kernels: 29.6 us -> 31.2 us  [shards(): pl.pallas_call(functools.partial(route_kernel, experts, groups), out_shap...]
where the time goes in v4:
time: 36.4 us; the launch traced here: 36.2 us
  Pallas kernels  35.6 us (98%)
  between operations  0.64 us (2%)
    pallas_call x1, Pallas kernels, shards(): pl.pallas_call(functools.partial(route_kernel, experts, groups), out_shap...  31.2 us
    pallas_call x1, Pallas kernels, shards(): pl.pallas_call(weight_kernel, out_shape=(jax.ShapeDtypeStruct((toks, widt...  4.36 us

profile of v4, /device:TPU:0, one launch (start us, length us, event | category | flops | bytes accessed | tf_op | source)
XLA Modules:
  0.0 36.2 jit_solution(10891122615672450585)
XLA Ops:
  0.6 31.2 %route.1 = (bf16[32,1664]{1,0:T(8,128)(2,1)}, bf16[32,1664]{1,0:T(8,128)(2,1)}, bf16[32,1024]{1,0:T(8,128)(2,1)}, bf16[32,1024]{1,0:T(8,128)(2,1)}, bf16[128,1664]{1,0:T(8,128)(2,1)}, /*index=5*/f32[8,1664]{1,0:T(8,128)}) custom-call(bf16[128,1664]{1,0:T(8,128)(2,1)} %tok_hbm.1, bf16[128,1664]{1,0:T(8,128)(2,1)} %cot_hbm.1, s32[1,128]{1,0:T(1,128)} %bitcast.10, ...), custom_call_target="tpu_custom_call" | custom-call | tf_op jit(solution)/shard_map/route/pallas_call | solution.py:451
  31.9 4.4 %weight_grads.1 = (bf16[128,1664]{1,0:T(8,128)(2,1)}, bf16[1,1664,1024]{2,1,0:T(8,128)(2,1)}, bf16[1,1024,1664]{2,1,0:T(8,128)(2,1)}, f32[8,1664]{1,0:T(8,128)}) custom-call(bf16[32,1664]{1,0:T(8,128)(2,1)} %get-tuple-element.14.x_hbm, bf16[32,1664]{1,0:T(8,128)(2,1)} %get-tuple-element.15.og_hbm, bf16[32,1024]{1,0:T(8,128)(2,1)} %get-tuple-element.16.act_hbm, ...), custom_call_target="tpu_custom_call" | custom-call | tf_op jit(solution)/shard_map/weight_grads/pallas_call | solution.py:512

commit v5 on v4

--- a/solution.py
+++ b/solution.py
@@ -88,6 +88,7 @@
     head = 2 * head_s.shape[2]
     back = ret_s.shape[2]
     chunk = term_s.shape[2]
+    back_pieces = -(-(width + LANES) // back)
 
     barrier = pltpu.get_barrier_semaphore()
     for step in range(1, experts):
@@ -279,14 +280,6 @@
         )
 
     head_sum = to_groups(row_columns(0, head), head_s, head_r, h_ss, h_rs)
-    g1, g2, g3 = split3(gate_part)
-    tail = row_columns(head, width)
-    tail.append(jnp.where(lane == 0, g1, jnp.where(lane == 1, g2, jnp.where(lane == 2, g3, 0.0))))
-    spare = head + 2 * tail_s.shape[2] - width - LANES
-    if spare:
-        tail.append(jnp.zeros((count, spare), F32))
-    tail_sum = to_groups(tail, tail_s, tail_r, r_ss, r_rs)
-
     fold_row, fold_col = iota((LANES, LANES), 0), iota((LANES, LANES), 1)
     fold = one_hot((fold_row % experts == fold_col) & (fold_row < 3 * experts))
     row_prob = nn(gate_lanes.astype(BF16), fold)
@@ -309,11 +302,33 @@
     term_r[pl.ds(me, 1)] = term_s[pl.ds(me, 1)]
     scatter = exchange("expert", experts, me, lambda peer: term_s.at[peer], term_r.at[me], t_ss, t_rs)
 
+    g1, g2, g3 = split3(gate_part)
+    tail = row_columns(head, width)
+    tail.append(jnp.where(lane == 0, g1, jnp.where(lane == 1, g2, jnp.where(lane == 2, g3, 0.0))))
+    spare = head + 2 * tail_s.shape[2] - width - LANES
+    if spare:
+        tail.append(jnp.zeros((count, spare), F32))
+    tail_sum = to_groups(tail, tail_s, tail_r, r_ss, r_rs)
+
     def over_blocks(kept):
         summed = kept[0].astype(F32)
         for group in range(1, groups):
             summed = summed + kept[group].astype(F32)
         return [summed[:capacity], summed[capacity:]]
+
+    arrive(scatter)
+    term_sum = term_r[0]
+    for part in range(1, experts):
+        term_sum = term_sum + term_r[part]
+    sum_r[pl.ds(my_group, 1)] = term_sum[None]
+    over_dp = exchange("dp", groups, my_group, lambda peer: sum_r.at[my_group], sum_r.at[my_group], s_ss, s_rs)
+
+    marks = [
+        jnp.where(seat_turned // SLOT == part, hit_turned, 0.0).astype(BF16)
+        for part in range(back_pieces)
+    ]
+    r1, r2, r3 = split3(router)
+    near = jnp.concatenate([r1, r2, r1, r3, r1, r2], axis=0).astype(BF16)
 
     arrive(head_sum)
     row_sides = over_blocks(head_r)
@@ -328,7 +343,6 @@
         axis=1,
     ).astype(BF16).astype(F32)
     returned = jnp.zeros((wide, back), F32)
-    back_pieces = -(-(width + LANES) // back)
     for part in range(back_pieces):
         low = part * back
         high = min(width + LANES, low + back)
@@ -340,20 +354,6 @@
     ret_s[...] = returned.astype(BF16).reshape(experts, SEG, back)
     ret_r[pl.ds(me, 1)] = ret_s[pl.ds(me, 1)]
     give_back = exchange("expert", experts, me, lambda peer: ret_s.at[peer], ret_r.at[me], b_ss, b_rs)
-
-    arrive(scatter)
-    term_sum = term_r[0]
-    for part in range(1, experts):
-        term_sum = term_sum + term_r[part]
-    sum_r[pl.ds(my_group, 1)] = term_sum[None]
-    over_dp = exchange("dp", groups, my_group, lambda peer: sum_r.at[my_group], sum_r.at[my_group], s_ss, s_rs)
-
-    marks = [
-        jnp.where(seat_turned // SLOT == part, hit_turned, 0.0).astype(BF16)
-        for part in range(back_pieces)
-    ]
-    r1, r2, r3 = split3(router)
-    near = jnp.concatenate([r1, r2, r1, r3, r1, r2], axis=0).astype(BF16)
 
     arrive(over_dp)
     final = sum_r[0]

time: 36.4 us -> 35.5 us (0.975)
  Pallas kernels: 35.6 us -> 34.7 us
    pallas_call x1, Pallas kernels: 31.2 us -> 30.3 us  [shards(): pl.pallas_call(functools.partial(route_kernel, experts, groups), out_shap...]
where the time goes in v5:
time: 35.5 us; the launch traced here: 35.3 us
  Pallas kernels  34.7 us (98%)
  between operations  0.64 us (2%)
    pallas_call x1, Pallas kernels, shards(): pl.pallas_call(functools.partial(route_kernel, experts, groups), out_shap...  30.3 us
    pallas_call x1, Pallas kernels, shards(): pl.pallas_call(weight_kernel, out_shape=(jax.ShapeDtypeStruct((toks, widt...  4.35 us

profile of v5, /device:TPU:0, one launch (start us, length us, event | category | flops | bytes accessed | tf_op | source)
XLA Modules:
  0.0 35.3 jit_solution(7573109230985317748)
XLA Ops:
  0.6 30.3 %route.1 = (bf16[32,1664]{1,0:T(8,128)(2,1)}, bf16[32,1664]{1,0:T(8,128)(2,1)}, bf16[32,1024]{1,0:T(8,128)(2,1)}, bf16[32,1024]{1,0:T(8,128)(2,1)}, bf16[128,1664]{1,0:T(8,128)(2,1)}, /*index=5*/f32[8,1664]{1,0:T(8,128)}) custom-call(bf16[128,1664]{1,0:T(8,128)(2,1)} %tok_hbm.1, bf16[128,1664]{1,0:T(8,128)(2,1)} %cot_hbm.1, s32[1,128]{1,0:T(1,128)} %bitcast.10, ...), custom_call_target="tpu_custom_call" | custom-call | tf_op jit(solution)/shard_map/route/pallas_call | solution.py:451
  31.0 4.4 %weight_grads.1 = (bf16[128,1664]{1,0:T(8,128)(2,1)}, bf16[1,1664,1024]{2,1,0:T(8,128)(2,1)}, bf16[1,1024,1664]{2,1,0:T(8,128)(2,1)}, f32[8,1664]{1,0:T(8,128)}) custom-call(bf16[32,1664]{1,0:T(8,128)(2,1)} %get-tuple-element.14.x_hbm, bf16[32,1664]{1,0:T(8,128)(2,1)} %get-tuple-element.15.og_hbm, bf16[32,1024]{1,0:T(8,128)(2,1)} %get-tuple-element.16.act_hbm, ...), custom_call_target="tpu_custom_call" | custom-call | tf_op jit(solution)/shard_map/weight_grads/pallas_call | solution.py:512

commit v6 on v5

--- a/solution.py
+++ b/solution.py
@@ -72,9 +72,9 @@
     experts, groups, tok_hbm, cot_hbm, cnt_hbm, pick_hbm, router_hbm, win_hbm, wout_hbm,
     x_hbm, og_hbm, act_hbm, pg_hbm, gt_hbm, gr_hbm,
     x_ref, og_ref, gt_ref, gr_ref, tok_ref, cot_ref, cnt_ref, pick_ref, router_ref, win, wout,
-    send, recv, gate_s, gate_r, pack_x, pack_d, act_ref, pg_ref, slope_ref, head_s, head_r, tail_s, tail_r, ret_s, ret_r,
+    send, recv, gate_s, gate_r, pack_x, pack_d, pack_g, act_ref, pg_ref, slope_ref, head_s, head_r, tail_s, tail_r, ret_s, ret_r,
     term_s, term_r, sum_r, fin_r,
-    in_sem, out_sem, d_ss, d_rs, g_ss, g_rs, x_ss, x_rs, y_ss, y_rs, h_ss, h_rs, r_ss, r_rs, b_ss, b_rs, t_ss, t_rs, s_ss, s_rs, f_ss, f_rs,
+    in_sem, out_sem, d_ss, d_rs, g_ss, g_rs, x_ss, x_rs, y_ss, y_rs, z_ss, z_rs, h_ss, h_rs, r_ss, r_rs, b_ss, b_rs, t_ss, t_rs, s_ss, s_rs, f_ss, f_rs,
 ):
     me = lax.axis_index("expert")
     my_group = lax.axis_index("dp")
@@ -221,14 +221,16 @@
     gather_x = exchange(
         "dp", groups, my_group, lambda peer: pack_x.at[my_group], pack_x.at[my_group], x_ss, x_rs
     )
+    pack_d[pl.ds(my_group, 1)] = folded(packed[capacity:])[None]
+    gather_d = exchange(
+        "dp", groups, my_group, lambda peer: pack_d.at[my_group], pack_d.at[my_group], y_ss, y_rs
+    )
     arrive(send_gates)
     gate_rows = nn(gate_block, gate_r[...].reshape(wide, LANES))
-    packed_d = [packed[capacity:, :width], gate_rows]
-    if whole > width + LANES:
-        packed_d.append(jnp.zeros((capacity, whole - width - LANES), F32))
-    pack_d[pl.ds(my_group, 1)] = folded(jnp.concatenate(packed_d, axis=1))[None]
-    gather_d = exchange(
-        "dp", groups, my_group, lambda peer: pack_d.at[my_group], pack_d.at[my_group], y_ss, y_rs
+    gate_rows = jnp.concatenate([gate_rows, jnp.zeros((capacity, LANES), F32)], axis=0)
+    pack_g[pl.ds(my_group, 1)] = gate_rows.astype(BF16)[None]
+    gather_g = exchange(
+        "dp", groups, my_group, lambda peer: pack_g.at[my_group], pack_g.at[my_group], z_ss, z_rs
     )
     load_in.wait()
     load_out.wait()
@@ -247,9 +249,9 @@
     stores[2].start()
 
     arrive(gather_d)
-    dy_full = unfolded(pack_d)
-    dy_wide = dy_full[:, :width]
-    gate_lanes = dy_full[:, width : width + LANES]
+    dy_wide = unfolded(pack_d)[:, :width]
+    arrive(gather_g)
+    gate_lanes = pack_g[...].astype(F32)[:, :capacity].reshape(count, LANES)
     lane = iota((count, LANES), 1)
     gate = jnp.sum(jnp.where(lane == me, gate_lanes, 0.0), axis=1, keepdims=True)
     dy_rows = dy_wide.astype(BF16)
@@ -389,7 +391,7 @@
     stores[5].start()
     for store in stores:
         store.wait()
-    for copies in (dispatch, send_gates, gather_x, gather_d, head_sum, tail_sum, give_back, scatter, over_dp, spread_out):
+    for copies in (dispatch, send_gates, gather_x, gather_d, gather_g, head_sum, tail_sum, give_back, scatter, over_dp, spread_out):
         for copy in copies:
             copy.wait_send()
 
@@ -477,6 +479,7 @@
             pltpu.VMEM((experts, SEG, LANES), BF16),
             pltpu.VMEM((groups, 2 * capacity, half), BF16),
             pltpu.VMEM((groups, 2 * capacity, half), BF16),
+            pltpu.VMEM((groups, 2 * capacity, LANES), BF16),
             pltpu.VMEM((count, hidden), BF16),
             pltpu.VMEM((count, hidden), BF16),
             pltpu.VMEM((count, hidden), F32),
@@ -494,6 +497,7 @@
             dma((6,)),
             over_e, over_e,
             over_e, over_e,
+            over_g, over_g,
             over_g, over_g,
             over_g, over_g,
             over_g, over_g,

time: 35.5 us -> 35.9 us (1.011)
  Pallas kernels: 34.7 us -> 35.1 us
    pallas_call x1, Pallas kernels: 30.3 us -> 30.7 us  [shards(): pl.pallas_call(functools.partial(route_kernel, experts, groups), out_shap...]
where the time goes in v6:
time: 35.9 us; the launch traced here: 35.7 us
  Pallas kernels  35.1 us (98%)
  between operations  0.64 us (2%)
    pallas_call x1, Pallas kernels, shards(): pl.pallas_call(functools.partial(route_kernel, experts, groups), out_shap...  30.7 us
    pallas_call x1, Pallas kernels, shards(): pl.pallas_call(weight_kernel, out_shape=(jax.ShapeDtypeStruct((toks, widt...  4.35 us

profile of v6, /device:TPU:0, one launch (start us, length us, event | category | flops | bytes accessed | tf_op | source)
XLA Modules:
  0.0 35.7 jit_solution(7801962000521861399)
XLA Ops:
  0.6 30.7 %route.1 = (bf16[32,1664]{1,0:T(8,128)(2,1)}, bf16[32,1664]{1,0:T(8,128)(2,1)}, bf16[32,1024]{1,0:T(8,128)(2,1)}, bf16[32,1024]{1,0:T(8,128)(2,1)}, bf16[128,1664]{1,0:T(8,128)(2,1)}, /*index=5*/f32[8,1664]{1,0:T(8,128)}) custom-call(bf16[128,1664]{1,0:T(8,128)(2,1)} %tok_hbm.1, bf16[128,1664]{1,0:T(8,128)(2,1)} %cot_hbm.1, s32[1,128]{1,0:T(1,128)} %bitcast.10, ...), custom_call_target="tpu_custom_call" | custom-call | tf_op jit(solution)/shard_map/route/pallas_call | solution.py:453
  31.4 4.4 %weight_grads.1 = (bf16[128,1664]{1,0:T(8,128)(2,1)}, bf16[1,1664,1024]{2,1,0:T(8,128)(2,1)}, bf16[1,1024,1664]{2,1,0:T(8,128)(2,1)}, f32[8,1664]{1,0:T(8,128)}) custom-call(bf16[32,1664]{1,0:T(8,128)(2,1)} %get-tuple-element.14.x_hbm, bf16[32,1664]{1,0:T(8,128)(2,1)} %get-tuple-element.15.og_hbm, bf16[32,1024]{1,0:T(8,128)(2,1)} %get-tuple-element.16.act_hbm, ...), custom_call_target="tpu_custom_call" | custom-call | tf_op jit(solution)/shard_map/weight_grads/pallas_call | solution.py:516
